TPU v7x, 1024 devices: a whole 4x8x16 slice. The times are simulated.
1024 devices in a mesh: user: 256 (over z, y, core), item: 4 (over x).
Axes of the slice: x: 4, y: 8, z: 16, core: 2. Of those that a mesh axis runs over, the one named last changes fastest.
Arguments:
- tiles: bfloat16 [49152, 128, 128], P(('user', 'item')), may hold values from -0.046875 to 0.046875
- tile_user: int32 [49152], P(('user', 'item')), may hold values from 0 to 3
- tile_item: int32 [49152], P(('user', 'item')), may hold values from 0 to 15
- tile_count: int32 [1024], P(('user', 'item')), may hold values from 1 to 48, as said below
- user_emb: bfloat16 [131072, 128], P('user'), may hold values from -6 to 6
- item_emb: bfloat16 [8192, 128], P('item'), may hold values from -6 to 6
Outputs:
- user_out: bfloat16 [131072, 128], P('user')
- item_out: bfloat16 [8192, 128], P(('item', 'user'))
Inputs may be any that keep to these rules, and one draw needn't show every extreme that they name: `tile_count`: every device has at least one live slot; some device has all 48 live.
All inputs are finite; a program needn't handle non-finite values.
Results may differ from a plain program's by a relative error of at most 0.014.
Values may be sent and summed in bfloat16 or wider, within the bound.
No kernel may reach another device: no remote copies, remote signals or barrier semaphores. Data moves between devices by JAX's collectives and lax.ppermute only.
A program may use at most 32 MiB of HBM per device.

v0:
```python
import jax
import jax.numpy as jnp
from jax import lax
from jax.sharding import PartitionSpec as P

DIM = 128
BLOCK = 128


def user_terms(tiles, tile_user, tile_item, live, item_src, user_count):
    item_count = item_src.shape[0] // BLOCK
    blocks = item_src.reshape(item_count, BLOCK, DIM)[tile_item]
    prod = jnp.einsum("tab,tbd->tad", tiles, blocks, preferred_element_type=jnp.float32)
    pick = (
        (tile_user[:, None] == jnp.arange(user_count, dtype=jnp.int32)[None, :]) & live[:, None]
    ).astype(jnp.float32)
    return jnp.einsum("tk,tad->kad", pick, prod).reshape(user_count * BLOCK, DIM)


def item_terms(tiles, tile_user, tile_item, live, user_src, item_count):
    user_count = user_src.shape[0] // BLOCK
    blocks = user_src.reshape(user_count, BLOCK, DIM)[tile_user]
    prod = jnp.einsum("tab,tad->tbd", tiles, blocks, preferred_element_type=jnp.float32)
    pick = (
        (tile_item[:, None] == jnp.arange(item_count, dtype=jnp.int32)[None, :]) & live[:, None]
    ).astype(jnp.float32)
    return jnp.einsum("tk,tbd->kbd", pick, prod).reshape(item_count * BLOCK, DIM)


def sum_users(partial_value):
    return lax.psum(partial_value.astype(jnp.bfloat16), "item").astype(jnp.float32)


def share_items(partial_value):
    return lax.psum_scatter(partial_value, "user", scatter_dimension=0, tiled=True)


def per_device(tiles, tile_user, tile_item, tile_count, user_emb, item_emb):
    live = jnp.arange(tiles.shape[0], dtype=jnp.int32) < tile_count[0]
    user_count = user_emb.shape[0] // BLOCK
    item_count = item_emb.shape[0] // BLOCK
    piece_rows = item_emb.shape[0] // lax.axis_size("user")
    piece_start = lax.axis_index("user") * piece_rows
    user_one = sum_users(
        user_terms(tiles, tile_user, tile_item, live, item_emb, user_count)
    ).astype(jnp.bfloat16)
    item_part = item_terms(tiles, tile_user, tile_item, live, user_emb, item_count)
    item_piece = share_items(item_part).astype(jnp.bfloat16)
    item_full = lax.all_gather(item_piece, "user", axis=0, tiled=True)
    user_two = sum_users(user_terms(tiles, tile_user, tile_item, live, item_full, user_count))
    item_two = share_items(item_terms(tiles, tile_user, tile_item, live, user_one, item_count))
    item_first = lax.dynamic_slice_in_dim(item_emb, piece_start, piece_rows, 0)
    user_out = (
        (user_emb.astype(jnp.float32) + user_one.astype(jnp.float32) + user_two) / 3.0
    ).astype(jnp.bfloat16)
    item_out = (
        (item_first.astype(jnp.float32) + item_piece.astype(jnp.float32) + item_two) / 3.0
    ).astype(jnp.bfloat16)
    return (user_out, item_out)


def solution(mesh):
    in_specs = (
        P(("user", "item"), None, None),
        P(("user", "item")),
        P(("user", "item")),
        P(("user", "item")),
        P("user", None),
        P("item", None),
    )
    out_specs = (P("user", None), P(("item", "user"), None))
    return jax.shard_map(
        per_device, mesh=mesh, in_specs=in_specs, out_specs=out_specs, check_vma=False
    )
```

profile of v0, /device:TPU:1, one launch (start us, length us, event | category | flops | bytes accessed | tf_op | source)
XLA Modules:
  0.0 1550.2 jit_solution(17978675900465933683)
XLA Ops:
  7.2 0.0 copy-start
  7.2 0.0 all-reduce.9.cloned.1.call-start
  7.2 0.8 compare_select_fusion
  8.0 1.8 gather_fusion.1
  9.8 0.0 copy-done
  9.8 1.8 convolution_bitcast_fusion.2
  11.6 0.0 copy-start.6
  11.6 2.0 copy.24
  14.3 0.0 copy-done.6
  14.4 0.3 fusion.4
  14.7 0.3 copy.25
  15.0 994.9 %all-reduce.10 = bf16[2048,128]{1,0:T(8,128)(2,1)S(1)} all-reduce(f32[2048,128]{1,0:T(8,128)S(1)} %bitcast.44), channel_id=2, replica_groups=mesh['user'=256,'item'=4] {'user'}, use_global_device_ids=true, to_apply=%region_1.0.clone | all-reduce | flops 262144 | bytes 1572864
  1009.9 0.0 copy-start.3
  1009.9 1.3 dynamic-slice
  1011.8 102.9 %all_gather.3 = bf16[2048,128]{1,0:T(8,128)(2,1)S(1)} all-gather(bf16[8,128]{1,0:T(8,128)(2,1)S(1)} %dynamic-slice_convert_fusion), channel_id=1, replica_groups=mesh['user'=256,'item'=4] {'user'}, dimensions={0}, use_global_device_ids=true | all-gather | bytes 526336 | tf_op jit(solution)/shard_map/all_gather | solution.py:49
  1114.7 2.0 gather_fusion.2
  1116.7 0.0 copy-done.3
  1116.7 3.8 convolution_bitcast_fusion.1
  1120.5 0.0 copy-start.5
  1120.5 2.0 copy.27
  1122.6 0.0 copy-done.5
  1122.6 0.3 convolution_convert_fusion
  1122.9 0.7 copy.28
  1123.6 1.9 gather_fusion
  1125.5 2.4 convolution_bitcast_fusion.3
  1127.9 2.0 copy.21
  1129.9 0.3 convolution_convert_fusion.1
  1130.2 0.7 copy.22
  1130.9 0.0 all-reduce.9.cloned.1.call-update
  1130.9 0.0 all-reduce.7.cloned.1.call-start
  1131.0 51.4 %all-reduce.9.cloned.1.call-done = (bf16[512,128]{1,0:T(8,128)(2,1)}, bf16[512,128]{1,0:T(8,128)(2,1)}) async-done(((bf16[512,128]{1,0:T(8,128)(2,1)}, bf16[512,128]{1,0:T(8,128)(2,1)}), (bf16[512,128]{1,0:T(8,128)(2,1)}, bf16[512,128]{1,0:T(8,128)(2,1)})) %all-reduce.9.cloned.1.call-update) | async-done | bytes 262160 | tf_op jit(solution)/shard_map/psum | solution.py:31
  1182.3 1.8 gather_fusion.3
  1184.1 1.8 convolution_bitcast_fusion
  1186.0 2.0 copy.30
  1188.0 0.3 fusion.2
  1188.3 0.0 copy-start.1
  1188.3 0.0 copy-start.2
  1188.3 0.0 copy-start.4
  1188.3 1.4 copy.31
  1189.7 0.0 all-reduce.7.cloned.1.call-update
  1189.7 0.0 copy-done.1
  1189.8 0.0 copy-done.2
  1189.8 0.0 copy-done.4
  1189.8 0.7 multiply_convert_fusion
  1190.5 351.6 %all-reduce.7.cloned.1.call-done = f32[2048,128]{1,0:T(8,128)} async-done(((f32[2048,128]{1,0:T(8,128)}), f32[2048,128]{1,0:T(8,128)}) %all-reduce.7.cloned.1.call-update) | async-done | bytes 1048592
  1542.1 1.3 fusion.7
  (5 shorter events, 0.0 us)
Async XLA Ops:
  7.2 2.6 copy-start
  7.2 1175.2 %all-reduce.9.cloned.1.call-start = ((), (), s32[]{:S(2)}) async-start(), calls=%async_computation.1 | async-start | bytes 524288 | tf_op jit(solution)/shard_map/psum | solution.py:31
  11.6 2.7 copy-start.6
  1009.9 106.8 %copy-start.3 = (bf16[2048,128]{1,0:T(8,128)(2,1)}, bf16[2048,128]{1,0:T(8,128)(2,1)S(1)}, u32[]{:S(2)}) copy-start(bf16[2048,128]{1,0:T(8,128)(2,1)S(1)} %all-reduce.10) | copy-start | bytes 1572868
  1120.5 2.1 copy-start.5
  1130.9 411.2 %all-reduce.7.cloned.1.call-start = ((), (), s32[]{:S(2)}) async-start(), calls=%async_computation | async-start | bytes 2097152
  1188.3 1.4 copy-start.1
  1188.3 1.4 copy-start.2
  1188.3 1.4 copy-start.4
Sparse Core Ops, SparseCore 0:
  1131.1 51.2 all-reduce.8
  1189.9 352.1 all-reduce.6
where the time goes:
time: 1550 us
  blocking collectives  1100 us (71%)
  waiting for transfers between devices  403 us (26%)
  local copies, waits for them, and re-layouts  19.8 us (1%)
  between operations  15.5 us (1%)
    unnamed x1, blocking collectives  995 us
    unnamed x3, waiting for transfers between devices  352 us
    all_gather x1, blocking collectives, per_device(): item_full = lax.all_gather(item_piece, 'user', axis=0, tiled=True)  103 us
    psum x1, waiting for transfers between devices, sum_users(): lax.psum(partial_value.astype(jnp.bfloat16), 'item').astype(jnp.float32)  51.4 us
  transfers between devices with their start and end apart: 2, of which 2 were waited for; matrix products, arithmetic and copies ran while one was open for 0% of the time, Pallas kernels for 0%

commit v1 on v0

v1 whole, which is shorter than its diff:
```python
import jax
import jax.numpy as jnp
from jax import lax
from jax.experimental import pallas as pl
from jax.experimental.pallas import tpu as pltpu
from jax.sharding import Mesh, PartitionSpec as P

DIM = 128
BLOCK = 128
F32 = jnp.float32
BF16 = jnp.bfloat16

ZH, ZL, Y, CORE = 4, 4, 8, 2
GROUP = ZL * Y
AXES = ("zh", "zl", "y", "core")

VMEM = pl.BlockSpec(memory_space=pltpu.VMEM)
SMEM = pl.BlockSpec(memory_space=pltpu.SMEM)
PARAMS = pltpu.CompilerParams(vmem_limit_bytes=40 * 1024 * 1024)


def first_kernel(tu_ref, ti_ref, count_ref, tiles_ref, item_ref, r_ref, part_ref, acc_ref):
    acc_ref[...] = jnp.zeros_like(acc_ref)

    def add(s, carry):
        rows = pl.ds(pl.multiple_of(tu_ref[s] * BLOCK, BLOCK), BLOCK)
        cols = pl.ds(pl.multiple_of(ti_ref[s] * BLOCK, BLOCK), BLOCK)
        acc_ref[rows, cols] += tiles_ref[s].astype(F32)
        return carry

    lax.fori_loop(0, count_ref[0], add, 0)
    r_ref[...] = acc_ref[...].astype(BF16)
    part = jnp.dot(r_ref[...], item_ref[...], preferred_element_type=F32).astype(BF16)
    for k in range(part_ref.shape[0]):
        part_ref[k] = part


def first_call(tile_user, tile_item, tile_count, tiles, item_emb, copies, users):
    items = item_emb.shape[0]
    return pl.pallas_call(
        first_kernel,
        out_shape=(
            jax.ShapeDtypeStruct((users, items), BF16),
            jax.ShapeDtypeStruct((copies, users, DIM), BF16),
        ),
        in_specs=[SMEM, SMEM, SMEM, VMEM, VMEM],
        out_specs=(VMEM, VMEM),
        scratch_shapes=[pltpu.VMEM((users, items), F32)],
        compiler_params=PARAMS,
        name="first",
    )(tile_user, tile_item, tile_count, tiles, item_emb)


def second_kernel(core_ref, r_ref, parts_ref, user_ref, one_ref, keep_ref, send_ref, two_ref):
    total = parts_ref[0].astype(F32)
    for k in range(1, parts_ref.shape[0]):
        total += parts_ref[k].astype(F32)
    one = total.astype(BF16)
    one_ref[...] = one
    both = jnp.concatenate([user_ref[...], one], axis=1)
    core = core_ref[0]
    half = ZH * ZL * BLOCK // CORE
    dims = (((0,), (0,)), ((), ()))
    out = lax.dot_general(r_ref[...], both, dims, preferred_element_type=F32)
    first = out[:, :DIM]
    two_ref[0] = first[:half].reshape(half, DIM)
    two_ref[1] = first[half:].reshape(half, DIM)
    for ref, side in ((keep_ref, core), (send_ref, 1 - core)):
        ref[:, 0] = two_ref[side].astype(BF16).reshape(GROUP, half // GROUP, DIM)
    second = out[:, DIM:].reshape(ZH, ZL, Y, CORE, 8, DIM)
    for zl in range(ZL):
        for y in range(Y):
            for c in range(CORE):
                two_ref[c, pl.ds((zl * Y + y) * 32, 32)] = jnp.concatenate(
                    [second[zh, zl, y, c] for zh in range(ZH)], axis=0
                )
    for ref, side in ((keep_ref, core), (send_ref, 1 - core)):
        ref[:, 1] = two_ref[side].astype(BF16).reshape(GROUP, half // GROUP, DIM)


def second_call(core, r, parts, user_emb):
    users, items = r.shape
    half = items // CORE
    piece = jax.ShapeDtypeStruct((GROUP, 2, half // GROUP, DIM), BF16)
    return pl.pallas_call(
        second_kernel,
        out_shape=(jax.ShapeDtypeStruct((users, DIM), BF16), piece, piece),
        in_specs=[SMEM, VMEM, VMEM, VMEM],
        out_specs=(VMEM, VMEM, VMEM),
        scratch_shapes=[pltpu.VMEM((CORE, half, DIM), F32)],
        compiler_params=PARAMS,
        name="second",
    )(core, r, parts, user_emb)


def third_kernel(at_ref, r_ref, one_ref, emb_ref, two_ref, part_ref, out_ref):
    part = jnp.dot(r_ref[...], one_ref[...], preferred_element_type=F32).astype(BF16)
    for k in range(part_ref.shape[0]):
        part_ref[k] = part
    start = pl.multiple_of(at_ref[0] * 16, 16)
    pair = one_ref[pl.ds(start, 16)].astype(F32) + emb_ref[pl.ds(start, 16)].astype(F32)
    mine = jnp.where(at_ref[1] == 0, pair[:8], pair[8:])
    out_ref[...] = ((mine + two_ref[...]) / 3.0).astype(BF16)


def third_call(at, r, item_one, item_emb, item_two, copies):
    users, items = r.shape
    return pl.pallas_call(
        third_kernel,
        out_shape=(
            jax.ShapeDtypeStruct((copies, users, DIM), BF16),
            jax.ShapeDtypeStruct((8, DIM), BF16),
        ),
        in_specs=[SMEM, VMEM, VMEM, VMEM, VMEM],
        out_specs=(VMEM, VMEM),
        compiler_params=PARAMS,
        name="third",
    )(at, r, item_one, item_emb, item_two)


def swap(x, axis):
    return lax.all_to_all(x, axis, 0, 0, tiled=True)


def per_device(tiles, tile_user, tile_item, tile_count, user_emb, item_emb):
    copies = lax.axis_size("item")
    users = user_emb.shape[0]
    core = lax.axis_index("core")
    r, part = first_call(tile_user, tile_item, tile_count, tiles, item_emb, copies, users)
    parts = swap(part, "item")
    user_one, keep, send = second_call(core[None], r, parts, user_emb)
    other = lax.ppermute(send, "core", [(0, 1), (1, 0)])
    chip = (keep.astype(F32) + other.astype(F32)).astype(BF16)
    got = swap(chip, ("zl", "y"))
    both = got.astype(F32).sum(axis=0).astype(BF16)
    wide = jnp.broadcast_to(both[0][None], (ZH, 32, DIM))
    got = swap(jnp.concatenate([wide, both[1].reshape(ZH, 8, DIM)], axis=1), "zh")
    total = got.astype(F32).sum(axis=0)
    mine = total[:32].astype(BF16)
    half = swap(jnp.broadcast_to(mine[None], (GROUP, 32, DIM)), ("zl", "y"))
    item_one = lax.all_gather(half.reshape(GROUP * 32, DIM), "core", axis=0, tiled=True)
    block = (lax.axis_index("zh") * ZL + lax.axis_index("zl")) * Y + lax.axis_index("y")
    at = jnp.stack([block, core]).astype(jnp.int32)
    part, item_out = third_call(at, r, item_one, item_emb, total[32:], copies)
    parts = swap(part, "item")
    user_two = parts.astype(F32).sum(axis=0)
    user_out = ((user_emb.astype(F32) + user_one.astype(F32) + user_two) / 3.0).astype(BF16)
    return user_out, item_out


def solution(mesh):
    fine = Mesh(mesh.devices.reshape(ZH, ZL, Y, CORE, -1), AXES + ("item",))
    every = P(AXES + ("item",))
    in_specs = (every, every, every, every, P(AXES, None), P("item", None))
    out_specs = (P(AXES, None), P(("item",) + AXES, None))
    return jax.shard_map(
        per_device, mesh=fine, in_specs=in_specs, out_specs=out_specs, check_vma=False
    )
```

time: 1550 us -> 120 us (0.08)
  blocking collectives: 1100 us -> 61.2 us
  waiting for transfers between devices: 403 us -> 18.7 us
  starting transfers between devices: 0.08 us -> 27.8 us
    unnamed x1 -> x0, blocking collectives: 995 us -> none
    unnamed x3 -> x0, waiting for transfers between devices: 352 us -> none
    all_gather x1, blocking collectives: 103 us -> 4.9 us  [per_device(): lax.all_gather(half.reshape(GROUP * 32, DIM), 'core', axis=0, tiled=True)]
    all_to_all x0 -> x3, blocking collectives: none -> 56.3 us  [swap(): return lax.all_to_all(x, axis, 0, 0, tiled=True)]
    psum x1 -> x0, waiting for transfers between devices: 51.4 us -> none  [sum_users(): lax.psum(partial_value.astype(jnp.bfloat16), 'item').astype(jnp.float32)]
    all_to_all x0 -> x2, waiting for transfers between devices: none -> 17.2 us  [swap(): return lax.all_to_all(x, axis, 0, 0, tiled=True)]
    ppermute x0 -> x1, starting transfers between devices: none -> 15.5 us  [per_device(): other = lax.ppermute(send, 'core', [(0, 1), (1, 0)])]
  transfers between devices with their start and end apart: 2 -> 3, of which waited for: 2 -> 3; matrix products, arithmetic and copies ran while one was open for 0% -> 0% of each run, Pallas kernels for 0% -> 0%
where the time goes in v1:
time: 120 us
  blocking collectives  61.2 us (51%)
  starting transfers between devices  27.8 us (23%)
  waiting for transfers between devices  18.7 us (16%)
  Pallas kernels  5.2 us (4%)
  local copies, waits for them, and re-layouts  4.52 us (4%)
  between operations  1.37 us (1%)
    all_to_all x3, blocking collectives, swap(): return lax.all_to_all(x, axis, 0, 0, tiled=True)  56.3 us
    all_to_all x2, waiting for transfers between devices, swap(): return lax.all_to_all(x, axis, 0, 0, tiled=True)  17.2 us
    ppermute x1, starting transfers between devices, per_device(): other = lax.ppermute(send, 'core', [(0, 1), (1, 0)])  15.5 us
    all_to_all x2, starting transfers between devices, swap(): return lax.all_to_all(x, axis, 0, 0, tiled=True)  12.2 us
    all_gather x1, blocking collectives, per_device(): lax.all_gather(half.reshape(GROUP * 32, DIM), 'core', axis=0, tiled=True)  4.9 us
    unnamed x12, local copies, waits for them, and re-layouts  3.76 us
    pallas_call x1, Pallas kernels, first_call(): pl.pallas_call(first_kernel, out_shape=(jax.ShapeDtypeStruct((users, item...  2.48 us
  transfers between devices with their start and end apart: 3, of which 3 were waited for; matrix products, arithmetic and copies ran while one was open for 0% of the time, Pallas kernels for 0%

profile of v1, /device:TPU:1, one launch (start us, length us, event | category | flops | bytes accessed | tf_op | source)
XLA Modules:
  0.0 120.0 jit_solution(5680614907834177429)
XLA Ops:
  1.3 0.0 copy-start
  1.3 1.0 copy-done
  2.3 0.0 copy-start.2
  2.3 1.4 %copy-done.2 = bf16[48,128,128]{2,1,0:T(8,128)(2,1)S(1)} copy-done((bf16[48,128,128]{2,1,0:T(8,128)(2,1)S(1)}, bf16[48,128,128]{2,1,0:T(8,128)(2,1)}, u32[]{:S(2)}) %copy-start.2) | copy-done | bytes 1572888
  3.7 0.0 copy-start.4
  3.7 0.7 copy-done.4
  4.4 0.0 copy-start.5
  4.4 0.7 copy-done.5
  5.0 0.0 copy-start.3
  5.0 2.5 %first.1 = (bf16[512,2048]{1,0:T(8,128)(2,1)S(1)}, bf16[4,512,128]{2,1,0:T(8,128)(2,1)}) custom-call(s32[48]{0:T(128)S(1)} %copy-done.4, s32[48]{0:T(128)S(1)} %copy-done.5, s32[1]{0:T(128)S(6)} %copy.8.count_ref, bf16[48,128,128]{2,1,0:T(8,128)(2,1)S(1)} %copy-done.2, bf16[2048,128]{1,0:T(8,128)(2,1)S(1)} %copy-done), custom_call_target="tpu_custom_call" | custom-call | tf_op jit(solution)/shard_map/first/pallas_call | solution.py:40
  7.5 5.1 %all-to-all-start = ((bf16[4,512,128]{2,1,0:T(8,128)(2,1)}), bf16[4,512,128]{2,1,0:T(8,128)(2,1)S(1)}, u32[]{:S(2)}, u32[]{:S(2)}) async-start(bf16[4,512,128]{2,1,0:T(8,128)(2,1)} %get-tuple-element.10), calls=%async_computation | async-start | bytes 1048576 | tf_op jit(solution)/shard_map/all_to_all | solution.py:122
  12.7 6.9 %all-to-all-done.parts_ref = bf16[4,512,128]{2,1,0:T(8,128)(2,1)S(1)} async-done(((bf16[4,512,128]{2,1,0:T(8,128)(2,1)}), bf16[4,512,128]{2,1,0:T(8,128)(2,1)S(1)}, u32[]{:S(2)}, u32[]{:S(2)}) %all-to-all-start) | async-done | bytes 524320 | tf_op jit(solution)/shard_map/all_to_all | solution.py:122
  19.6 0.0 copy-done.3
  19.6 1.0 second.1
  20.6 15.5 %collective-permute-start = (bf16[32,2,32,128]{3,2,1,0:T(8,128)(2,1)S(1)}, bf16[32,2,32,128]{3,2,1,0:T(8,128)(2,1)S(1)}, u32[]{:S(2)}, u32[]{:S(2)}) collective-permute-start(bf16[32,2,32,128]{3,2,1,0:T(8,128)(2,1)S(1)} %get-tuple-element.13), channel_id=1, source_target_pairs={{0,4},{4,0},{1,5},{5,1},{2,6},{6,2},{3,7},{7,3},{8,12},{12,8},{9,1... | collective-permute-start | bytes 1572872 | tf_op jit(solution)/shard_map/ppermute | solution.py:132
  36.1 1.5 %collective-permute-done = bf16[32,2,32,128]{3,2,1,0:T(8,128)(2,1)S(1)} collective-permute-done((bf16[32,2,32,128]{3,2,1,0:T(8,128)(2,1)S(1)}, bf16[32,2,32,128]{3,2,1,0:T(8,128)(2,1)S(1)}, u32[]{:S(2)}, u32[]{:S(2)}) %collective-permute-start) | collective-permute-done | bytes 524320 | tf_op jit(solution)/shard_map/ppermute | solution.py:132
  37.6 0.2 add_convert_fusion
  37.8 0.0 copy-start.1
  37.8 18.7 %all_to_all.25 = bf16[32,2,32,128]{3,2,1,0:T(8,128)(2,1)S(1)} all-to-all(bf16[32,2,32,128]{3,2,1,0:T(8,128)(2,1)S(1)} %add_convert_fusion), channel_id=1, replica_groups=mesh['zh'=4,'zl'=4,'y'=8,'core'=2,'item'=4] {'zl','y'}, dimensions={0} | all-to-all | bytes 1048576 | tf_op jit(solution)/shard_map/all_to_all | solution.py:122
  56.6 0.1 reduce_sum.30
  56.7 26.0 %all_to_all.26 = bf16[4,40,128]{2,1,0:T(8,128)(2,1)S(1)} all-to-all(bf16[4,40,128]{2,1,0:T(8,128)(2,1)S(1)} %pad_maximum_fusion), channel_id=1, replica_groups=mesh['zh'=4,'zl'=4,'y'=8,'core'=2,'item'=4] {'zh'}, dimensions={0} | all-to-all | bytes 81920 | tf_op jit(solution)/shard_map/all_to_all | solution.py:122
  82.7 0.7 broadcast_in_dim.19
  83.5 7.1 %all-to-all-start.3 = ((bf16[32,32,128]{2,1,0:T(8,128)(2,1)}), bf16[32,32,128]{2,1,0:T(8,128)(2,1)S(1)}, u32[]{:S(2)}, u32[]{:S(2)}) async-start(bf16[32,32,128]{2,1,0:T(8,128)(2,1)} %broadcast_in_dim.19), calls=%async_computation.3 | async-start | bytes 524288 | tf_op jit(solution)/shard_map/all_to_all | solution.py:122
  90.6 0.1 pad_add_fusion.at_ref
  90.7 10.3 %all-to-all-done.3 = bf16[32,32,128]{2,1,0:T(8,128)(2,1)S(1)} async-done(((bf16[32,32,128]{2,1,0:T(8,128)(2,1)}), bf16[32,32,128]{2,1,0:T(8,128)(2,1)S(1)}, u32[]{:S(2)}, u32[]{:S(2)}) %all-to-all-start.3) | async-done | bytes 262176 | tf_op jit(solution)/shard_map/all_to_all | solution.py:122
  100.9 4.9 %all_gather.3.one_ref = bf16[2048,128]{1,0:T(8,128)(2,1)S(1)} all-gather(bf16[1024,128]{1,0:T(8,128)(2,1)S(1)} %bitcast.7), channel_id=1, replica_groups=mesh['zh'=4,'zl'=4,'y'=8,'core'=2,'item'=4] {'core'}, dimensions={0}, use_global_device_ids=true | all-gather | bytes 786432 | tf_op jit(solution)/shard_map/all_gather | solution.py:141
  105.8 0.0 copy-done.1
  105.8 1.7 %third.1 = (bf16[4,512,128]{2,1,0:T(8,128)(2,1)S(1)}, bf16[8,128]{1,0:T(8,128)(2,1)}) custom-call(s32[2]{0:T(128)S(1)} %pad_add_fusion.at_ref, bf16[512,2048]{1,0:T(8,128)(2,1)S(1)} %get-tuple-element.9.r_ref, bf16[2048,128]{1,0:T(8,128)(2,1)S(1)} %all_gather.3.one_ref, bf16[2048,128]{1,0:T(8,128)(2,1)S(1)} %copy-done.1, f32[8,128]{1,0:T(8,128)S(1)} %slice.20.two_ref), custom_call_target="tpu_custom_call" | custom-call | tf_op jit(solution)/shard_map/third/pallas_call | solution.py:108
  107.6 11.6 %all_to_all.27 = bf16[4,512,128]{2,1,0:T(8,128)(2,1)S(1)} all-to-all(bf16[4,512,128]{2,1,0:T(8,128)(2,1)S(1)} %get-tuple-element.14), channel_id=1, replica_groups=mesh['zh'=4,'zl'=4,'y'=8,'core'=2,'item'=4] {'item'}, dimensions={0} | all-to-all | bytes 1048576 | tf_op jit(solution)/shard_map/all_to_all | solution.py:122
  119.2 0.1 convert_reduce_fusion
  119.3 0.7 multiply_convert_fusion
  (6 shorter events, 0.0 us)
Async XLA Ops:
  1.3 1.0 copy-start
  2.3 1.4 %copy-start.2 = (bf16[48,128,128]{2,1,0:T(8,128)(2,1)S(1)}, bf16[48,128,128]{2,1,0:T(8,128)(2,1)}, u32[]{:S(2)}) copy-start(bf16[48,128,128]{2,1,0:T(8,128)(2,1)} %tiles_ref.1) | copy-start | bytes 4718596
  3.7 0.7 copy-start.4
  4.4 0.7 copy-start.5
  5.0 14.6 %copy-start.3 = (bf16[512,128]{1,0:T(8,128)(2,1)S(1)}, bf16[512,128]{1,0:T(8,128)(2,1)}, u32[]{:S(2)}) copy-start(bf16[512,128]{1,0:T(8,128)(2,1)} %user_ref.1) | copy-start | bytes 393220
  7.5 12.1 %all-to-all-start = ((bf16[4,512,128]{2,1,0:T(8,128)(2,1)}), bf16[4,512,128]{2,1,0:T(8,128)(2,1)S(1)}, u32[]{:S(2)}, u32[]{:S(2)}) async-start(bf16[4,512,128]{2,1,0:T(8,128)(2,1)} %get-tuple-element.10), calls=%async_computation | async-start | bytes 1048576 | tf_op jit(solution)/shard_map/all_to_all | solution.py:122
  20.6 17.1 %collective-permute-start = (bf16[32,2,32,128]{3,2,1,0:T(8,128)(2,1)S(1)}, bf16[32,2,32,128]{3,2,1,0:T(8,128)(2,1)S(1)}, u32[]{:S(2)}, u32[]{:S(2)}) collective-permute-start(bf16[32,2,32,128]{3,2,1,0:T(8,128)(2,1)S(1)} %get-tuple-element.13), channel_id=1, source_target_pairs={{0,4},{4,0},{1,5},{5,1},{2,6},{6,2},{3,7},{7,3},{8,12},{12,8},{9,1... | collective-permute-start | bytes 1572872 | tf_op jit(solution)/shard_map/ppermute | solution.py:132
  37.8 68.0 %copy-start.1 = (bf16[2048,128]{1,0:T(8,128)(2,1)S(1)}, bf16[2048,128]{1,0:T(8,128)(2,1)}, u32[]{:S(2)}) copy-start(bf16[2048,128]{1,0:T(8,128)(2,1)} %emb_ref.1) | copy-start | bytes 1572868
  83.5 17.5 %all-to-all-start.3 = ((bf16[32,32,128]{2,1,0:T(8,128)(2,1)}), bf16[32,32,128]{2,1,0:T(8,128)(2,1)S(1)}, u32[]{:S(2)}, u32[]{:S(2)}) async-start(bf16[32,32,128]{2,1,0:T(8,128)(2,1)} %broadcast_in_dim.19), calls=%async_computation.3 | async-start | bytes 524288 | tf_op jit(solution)/shard_map/all_to_all | solution.py:122

commit v2 on v1

v2 whole, which is shorter than its diff:
```python
import jax
import jax.numpy as jnp
from jax import lax
from jax.experimental import pallas as pl
from jax.experimental.pallas import tpu as pltpu
from jax.sharding import Mesh, PartitionSpec as P

DIM = 128
BLOCK = 128
F32 = jnp.float32
BF16 = jnp.bfloat16

ZH, ZL, Y, CORE = 8, 2, 8, 2
GROUP = ZL * Y
AXES = ("zh", "zl", "y", "core")

VMEM = pl.BlockSpec(memory_space=pltpu.VMEM)
SMEM = pl.BlockSpec(memory_space=pltpu.SMEM)
HBM = pl.BlockSpec(memory_space=pltpu.HBM)
PARAMS = pltpu.CompilerParams(vmem_limit_bytes=32 * 1024 * 1024)
FIRST_DIMS = (((0,), (0,)), ((), ()))


def first_kernel(count_ref, tu_hbm, ti_hbm, tiles_hbm, item_hbm, r_ref, part_ref,
                 tu_ref, ti_ref, head_ref, next_ref, twice_ref,
                 tiles_ref, item_ref, sems):
    slots = tiles_hbm.shape[0]
    row_blocks, col_blocks = r_ref.shape[0] // BLOCK, r_ref.shape[1] // BLOCK
    small = [
        pltpu.make_async_copy(tu_hbm, tu_ref, sems.at[0]),
        pltpu.make_async_copy(ti_hbm, ti_ref, sems.at[1]),
    ]
    tiles = pltpu.make_async_copy(tiles_hbm, tiles_ref.at[pl.ds(0, slots)], sems.at[2])
    items = pltpu.make_async_copy(item_hbm, item_ref, sems.at[3])
    for copy in small + [tiles, items]:
        copy.start()
    tiles_ref[slots] = jnp.zeros((BLOCK, BLOCK), BF16)
    for block in range(row_blocks * col_blocks):
        head_ref[block] = slots
    next_ref[slots] = -1
    for copy in small:
        copy.wait()

    def place(s, found):
        block = tu_ref[s] * col_blocks + ti_ref[s]
        before = head_ref[block]
        again = next_ref[before] == slots
        next_ref[s] = before
        head_ref[block] = s
        twice_ref[found] = block
        return found + again.astype(jnp.int32)

    found = lax.fori_loop(0, count_ref[0], place, jnp.int32(0))
    tiles.wait()
    for u in range(row_blocks):
        for i in range(col_blocks):
            tile = tiles_ref[head_ref[u * col_blocks + i]]
            r_ref[u * BLOCK : (u + 1) * BLOCK, i * BLOCK : (i + 1) * BLOCK] = tile

    def gather(k, carry):
        block = twice_ref[k]
        start = head_ref[block]
        _, total = lax.while_loop(
            lambda at: at[0] != slots,
            lambda at: (next_ref[at[0]], at[1] + tiles_ref[at[0]].astype(F32)),
            (next_ref[start], tiles_ref[start].astype(F32)),
        )
        rows = pl.ds(pl.multiple_of(block // col_blocks * BLOCK, BLOCK), BLOCK)
        cols = pl.ds(pl.multiple_of(block % col_blocks * BLOCK, BLOCK), BLOCK)
        r_ref[rows, cols] = total.astype(BF16)
        return carry

    lax.fori_loop(0, found, gather, 0)
    items.wait()
    part = jnp.dot(r_ref[...], item_ref[...], preferred_element_type=F32)
    part_ref[...] = part.astype(BF16)


def first_call(tile_user, tile_item, tile_count, tiles, item_emb, users):
    items, slots = item_emb.shape[0], tiles.shape[0]
    blocks = (users // BLOCK) * (items // BLOCK)
    inputs = (tile_user, tile_item, tiles, item_emb)
    return pl.pallas_call(
        first_kernel,
        out_shape=(
            jax.ShapeDtypeStruct((users, items), BF16),
            jax.ShapeDtypeStruct((users, DIM), BF16),
        ),
        in_specs=[SMEM] + [HBM] * 4,
        out_specs=(VMEM, VMEM),
        scratch_shapes=[
            pltpu.SMEM((slots,), jnp.int32),
            pltpu.SMEM((slots,), jnp.int32),
            pltpu.SMEM((blocks,), jnp.int32),
            pltpu.SMEM((slots + 1,), jnp.int32),
            pltpu.SMEM((slots + 1,), jnp.int32),
            pltpu.VMEM((slots + 1, BLOCK, BLOCK), BF16),
            pltpu.VMEM(item_emb.shape, BF16),
            pltpu.SemaphoreType.DMA((4,)),
        ],
        compiler_params=PARAMS,
        name="first",
    )(tile_count, *(pltpu.with_memory_space_constraint(x, pltpu.HBM) for x in inputs))


def second_kernel(r_ref, parts_ref, user_ref, one_ref, keep_ref, send_ref, two_ref):
    total = parts_ref[0].astype(F32)
    for k in range(1, parts_ref.shape[0]):
        total += parts_ref[k].astype(F32)
    one = total.astype(BF16)
    one_ref[...] = one
    both = jnp.concatenate([user_ref[...], one], axis=1)
    back = lax.dot_general(r_ref[...], both, FIRST_DIMS, preferred_element_type=F32)
    two_ref[:, :, 0] = back[:, :DIM].astype(BF16).reshape(CORE, GROUP, -1, DIM)
    back = back[:, DIM:].reshape(ZH, ZL, Y, CORE, 8, DIM)
    for zl in range(ZL):
        for y in range(Y):
            for c in range(CORE):
                rows = jnp.concatenate([back[zh, zl, y, c] for zh in range(ZH)], axis=0)
                two_ref[c, zl * Y + y, 1] = rows.astype(BF16)
    core = lax.axis_index("core")
    keep_ref[...] = two_ref[core]
    send_ref[...] = two_ref[1 - core]


def second_call(r, parts, user_emb):
    users, items = r.shape
    piece = jax.ShapeDtypeStruct((GROUP, 2, items // CORE // GROUP, DIM), BF16)
    return pl.pallas_call(
        second_kernel,
        out_shape=(jax.ShapeDtypeStruct((users, DIM), BF16), piece, piece),
        in_specs=[VMEM, VMEM, VMEM],
        out_specs=(VMEM, VMEM, VMEM),
        scratch_shapes=[pltpu.VMEM((CORE,) + piece.shape, BF16)],
        compiler_params=PARAMS,
        name="second",
    )(r, parts, user_emb)


def spread_kernel(got_ref, out_ref, two_ref):
    total = got_ref[0].astype(F32)
    for k in range(1, got_ref.shape[0]):
        total += got_ref[k].astype(F32)
    rows = out_ref.shape[1]
    one = total[:rows].astype(BF16)
    for k in range(out_ref.shape[0]):
        out_ref[k] = one
    two_ref[...] = total[rows : rows + two_ref.shape[0]]


def spread_call(got, rows):
    return pl.pallas_call(
        spread_kernel,
        out_shape=(
            jax.ShapeDtypeStruct((GROUP, rows, DIM), BF16),
            jax.ShapeDtypeStruct((8, DIM), F32),
        ),
        in_specs=[VMEM],
        out_specs=(VMEM, VMEM),
        compiler_params=PARAMS,
        name="spread",
    )(got)


def third_kernel(r_ref, one_ref, emb_ref, two_ref, part_ref, out_ref):
    part = jnp.dot(r_ref[...], one_ref[...], preferred_element_type=F32)
    part_ref[...] = part.astype(BF16)
    block = (lax.axis_index("zh") * ZL + lax.axis_index("zl")) * Y + lax.axis_index("y")
    rows = pl.ds(pl.multiple_of(block * 16, 16), 16)
    pair = one_ref[rows].astype(F32) + emb_ref[rows].astype(F32)
    mine = jnp.where(lax.axis_index("core") == 0, pair[:8], pair[8:])
    out_ref[...] = ((mine + two_ref[...]) / 3.0).astype(BF16)


def third_call(r, item_one, item_emb, item_two):
    users, items = r.shape
    return pl.pallas_call(
        third_kernel,
        out_shape=(
            jax.ShapeDtypeStruct((users, DIM), BF16),
            jax.ShapeDtypeStruct((8, DIM), BF16),
        ),
        in_specs=[VMEM, VMEM, VMEM, VMEM],
        out_specs=(VMEM, VMEM),
        compiler_params=PARAMS,
        name="third",
    )(r, item_one, item_emb, item_two)


def swap(x, axis):
    return lax.all_to_all(x, axis, 0, 0, tiled=True)


def add_up(x):
    return x.astype(F32).sum(axis=0)


def per_device(tiles, tile_user, tile_item, tile_count, user_emb, item_emb):
    users = user_emb.shape[0]
    r, part = first_call(tile_user, tile_item, tile_count, tiles, item_emb, users)
    user_one, keep, send = second_call(r, lax.all_gather(part, "item", axis=0), user_emb)
    other = lax.ppermute(send, "core", [(0, 1), (1, 0)])
    chip = (keep.astype(F32) + other.astype(F32)).astype(BF16)
    both = add_up(swap(chip, ("zl", "y"))).astype(BF16)
    rows = both.shape[1]
    wide = jnp.broadcast_to(both[0][None], (ZH, rows, DIM))
    got = swap(jnp.concatenate([wide, both[1].reshape(ZH, -1, DIM)], axis=1), "zh")
    spread, item_two = spread_call(got, rows)
    half = swap(spread, ("zl", "y"))
    item_one = lax.all_gather(half.reshape(-1, DIM), "core", axis=0, tiled=True)
    part, item_out = third_call(r, item_one, item_emb, item_two)
    parts = lax.all_gather(part, "item", axis=0)
    user_out = ((user_emb.astype(F32) + user_one.astype(F32) + add_up(parts)) / 3.0).astype(BF16)
    return user_out, item_out


def solution(mesh):
    fine = Mesh(mesh.devices.reshape(ZH, ZL, Y, CORE, -1), AXES + ("item",))
    every = P(AXES + ("item",))
    in_specs = (every, every, every, every, P(AXES, None), P("item", None))
    out_specs = (P(AXES, None), P(("item",) + AXES, None))
    return jax.shard_map(
        per_device, mesh=fine, in_specs=in_specs, out_specs=out_specs, check_vma=False
    )
```

time: 120 us -> 113 us (0.942)
  the two profiles are of different devices: /device:TPU:1 before, /device:TPU:10 now
where the time goes in v2:
time: 113 us
  blocking collectives  102 us (90%)
  Pallas kernels  5.07 us (4%)
  starting transfers between devices  1.92 us (2%)
  waiting for transfers between devices  1.88 us (2%)
  between operations  1.39 us (1%)
    all_to_all x3, blocking collectives, swap(): return lax.all_to_all(x, axis, 0, 0, tiled=True)  72.3 us
    all_gather x1, blocking collectives, per_device(): lax.all_gather(part, 'item', axis=0)  13.7 us
    all_gather x1, blocking collectives, per_device(): parts = lax.all_gather(part, 'item', axis=0)  13.4 us
    pallas_call x1, Pallas kernels, first_call(): pl.pallas_call(first_kernel, out_shape=(jax.ShapeDtypeStruct((users, item...  2.7 us
  transfers between devices with their start and end apart: 1, of which 1 were waited for; matrix products, arithmetic and copies ran while one was open for 0% of the time, Pallas kernels for 0%

profile of v2, /device:TPU:10, one launch (start us, length us, event | category | flops | bytes accessed | tf_op | source)
XLA Modules:
  0.0 112.9 jit_solution(17949658789697212931)
XLA Ops:
  0.6 0.0 copy-start.1
  1.3 2.7 %first.1 = (bf16[512,2048]{1,0:T(8,128)(2,1)S(1)}, bf16[512,128]{1,0:T(8,128)(2,1)S(1)}) custom-call(s32[1]{0:T(128)S(6)} %copy.8.count_ref, s32[48]{0:T(128)} %tu_hbm.1, s32[48]{0:T(128)} %ti_hbm.1, bf16[48,128,128]{2,1,0:T(8,128)(2,1)} %tiles_hbm.1, bf16[2048,128]{1,0:T(8,128)(2,1)} %emb_ref.1), custom_call_target="tpu_custom_call" | custom-call | tf_op jit(solution)/shard_map/first/pallas_call | solution.py:83
  4.0 13.7 %all-gather = bf16[2048,128]{1,0:T(8,128)(2,1)S(1)} all-gather(bf16[512,128]{1,0:T(8,128)(2,1)S(1)} %get-tuple-element.12), channel_id=2, replica_groups=mesh['zh'=8,'zl'=2,'y'=8,'core'=2,'item'=4] {'item'}, dimensions={0}, use_global_device_ids=true | all-gather | bytes 655360 | tf_op jit(solution)/shard_map/all_gather | solution.py:201
  17.7 0.0 copy-done.1
  17.7 1.1 %second.1 = (bf16[512,128]{1,0:T(8,128)(2,1)S(1)}, bf16[16,2,64,128]{3,2,1,0:T(8,128)(2,1)S(1)}, bf16[16,2,64,128]{3,2,1,0:T(8,128)(2,1)S(1)}) custom-call(bf16[512,2048]{1,0:T(8,128)(2,1)S(1)} %get-tuple-element.11.r_ref, bf16[4,512,128]{2,1,0:T(8,128)(2,1)S(1)} %bitcast.8, bf16[512,128]{1,0:T(8,128)(2,1)S(1)} %copy-done.1), custom_call_target="tpu_custom_call" | custom-call | tf_op jit(solution)/shard_map/second/pallas_call | solution.py:129
  18.8 1.9 %collective-permute-start = (bf16[16,2,64,128]{3,2,1,0:T(8,128)(2,1)S(1)}, bf16[16,2,64,128]{3,2,1,0:T(8,128)(2,1)S(1)}, u32[]{:S(2)}, u32[]{:S(2)}) collective-permute-start(bf16[16,2,64,128]{3,2,1,0:T(8,128)(2,1)S(1)} %get-tuple-element.15), channel_id=1, source_target_pairs={{0,4},{4,0},{1,5},{5,1},{2,6},{6,2},{3,7},{7,3},{8,12},{12,8},{9,1... | collective-permute-start | bytes 1572872 | tf_op jit(solution)/shard_map/ppermute | solution.py:202
  20.8 1.9 %collective-permute-done = bf16[16,2,64,128]{3,2,1,0:T(8,128)(2,1)S(1)} collective-permute-done((bf16[16,2,64,128]{3,2,1,0:T(8,128)(2,1)S(1)}, bf16[16,2,64,128]{3,2,1,0:T(8,128)(2,1)S(1)}, u32[]{:S(2)}, u32[]{:S(2)}) %collective-permute-start) | collective-permute-done | bytes 524320 | tf_op jit(solution)/shard_map/ppermute | solution.py:202
  22.6 0.2 add_convert_fusion
  22.8 0.0 copy-start
  22.9 28.3 %all_to_all.15 = bf16[16,2,64,128]{3,2,1,0:T(8,128)(2,1)S(1)} all-to-all(bf16[16,2,64,128]{3,2,1,0:T(8,128)(2,1)S(1)} %add_convert_fusion), channel_id=1, replica_groups=mesh['zh'=8,'zl'=2,'y'=8,'core'=2,'item'=4] {'zl','y'}, dimensions={0} | all-to-all | bytes 1048576 | tf_op jit(solution)/shard_map/all_to_all | solution.py:191
  51.1 0.1 reduce_sum.21
  51.3 30.9 %all_to_all.16.got_ref = bf16[8,72,128]{2,1,0:T(8,128)(2,1)S(1)} all-to-all(bf16[8,72,128]{2,1,0:T(8,128)(2,1)S(1)} %pad_maximum_fusion), channel_id=1, replica_groups=mesh['zh'=8,'zl'=2,'y'=8,'core'=2,'item'=4] {'zh'}, dimensions={0} | all-to-all | bytes 294912 | tf_op jit(solution)/shard_map/all_to_all | solution.py:191
  82.2 13.2 %all_to_all.17 = bf16[16,64,128]{2,1,0:T(8,128)(2,1)S(1)} all-to-all(bf16[16,64,128]{2,1,0:T(8,128)(2,1)S(1)} %get-tuple-element.16), channel_id=1, replica_groups=mesh['zh'=8,'zl'=2,'y'=8,'core'=2,'item'=4] {'zl','y'}, dimensions={0} | all-to-all | bytes 524288 | tf_op jit(solution)/shard_map/all_to_all | solution.py:191
  95.4 2.2 %all_gather.17.one_ref = bf16[2048,128]{1,0:T(8,128)(2,1)S(1)} all-gather(bf16[1024,128]{1,0:T(8,128)(2,1)S(1)} %bitcast.10), channel_id=1, replica_groups=mesh['zh'=8,'zl'=2,'y'=8,'core'=2,'item'=4] {'core'}, dimensions={0}, use_global_device_ids=true | all-gather | bytes 786432 | tf_op jit(solution)/shard_map/all_gather | solution.py:210
  97.5 0.0 copy-done
  97.5 1.2 %third.1 = (bf16[512,128]{1,0:T(8,128)(2,1)S(1)}, bf16[8,128]{1,0:T(8,128)(2,1)}) custom-call(bf16[512,2048]{1,0:T(8,128)(2,1)S(1)} %get-tuple-element.11.r_ref, bf16[2048,128]{1,0:T(8,128)(2,1)S(1)} %all_gather.17.one_ref, bf16[2048,128]{1,0:T(8,128)(2,1)S(1)} %copy-done, f32[8,128]{1,0:T(8,128)S(1)} %get-tuple-element.17.two_ref), custom_call_target="tpu_custom_call" | custom-call | tf_op jit(solution)/shard_map/third/pallas_call | solution.py:177
  98.8 13.4 %all-gather.1 = bf16[2048,128]{1,0:T(8,128)(2,1)S(1)} all-gather(bf16[512,128]{1,0:T(8,128)(2,1)S(1)} %get-tuple-element.18), channel_id=3, replica_groups=mesh['zh'=8,'zl'=2,'y'=8,'core'=2,'item'=4] {'item'}, dimensions={0}, use_global_device_ids=true | all-gather | bytes 655360 | tf_op jit(solution)/shard_map/all_gather | solution.py:212
  112.1 0.1 convert_reduce_fusion
  112.2 0.7 multiply_convert_fusion
  (4 shorter events, 0.1 us)
Async XLA Ops:
  0.6 17.1 %copy-start.1 = (bf16[512,128]{1,0:T(8,128)(2,1)S(1)}, bf16[512,128]{1,0:T(8,128)(2,1)}, u32[]{:S(2)}) copy-start(bf16[512,128]{1,0:T(8,128)(2,1)} %user_ref.1) | copy-start | bytes 393220
  18.8 3.8 %collective-permute-start = (bf16[16,2,64,128]{3,2,1,0:T(8,128)(2,1)S(1)}, bf16[16,2,64,128]{3,2,1,0:T(8,128)(2,1)S(1)}, u32[]{:S(2)}, u32[]{:S(2)}) collective-permute-start(bf16[16,2,64,128]{3,2,1,0:T(8,128)(2,1)S(1)} %get-tuple-element.15), channel_id=1, source_target_pairs={{0,4},{4,0},{1,5},{5,1},{2,6},{6,2},{3,7},{7,3},{8,12},{12,8},{9,1... | collective-permute-start | bytes 1572872 | tf_op jit(solution)/shard_map/ppermute | solution.py:202
  22.8 74.7 %copy-start = (bf16[2048,128]{1,0:T(8,128)(2,1)S(1)}, bf16[2048,128]{1,0:T(8,128)(2,1)}, u32[]{:S(2)}) copy-start(bf16[2048,128]{1,0:T(8,128)(2,1)} %emb_ref.1) | copy-start | bytes 1572868

commit v3 on v2

v3 whole, which is shorter than its diff:
```python
import jax
import jax.numpy as jnp
from jax import lax
from jax.experimental import pallas as pl
from jax.experimental.pallas import tpu as pltpu
from jax.sharding import Mesh, PartitionSpec as P

DIM = 128
BLOCK = 128
F32 = jnp.float32
BF16 = jnp.bfloat16

ZH, ZL, Y, CORE = 8, 2, 8, 2
GROUP = ZL * Y
AXES = ("zh", "zl", "y", "core")

VMEM = pl.BlockSpec(memory_space=pltpu.VMEM)
SMEM = pl.BlockSpec(memory_space=pltpu.SMEM)
HBM = pl.BlockSpec(memory_space=pltpu.HBM)
PARAMS = pltpu.CompilerParams(vmem_limit_bytes=32 * 1024 * 1024)
FIRST_DIMS = (((0,), (0,)), ((), ()))


def first_kernel(count_ref, tu_hbm, ti_hbm, tiles_hbm, item_hbm, user_hbm, r_ref, part_ref, user_ref,
                 tu_ref, ti_ref, head_ref, next_ref, twice_ref,
                 tiles_ref, item_ref, sems):
    slots = tiles_hbm.shape[0]
    row_blocks, col_blocks = r_ref.shape[0] // BLOCK, r_ref.shape[1] // BLOCK
    small = [
        pltpu.make_async_copy(tu_hbm, tu_ref, sems.at[0]),
        pltpu.make_async_copy(ti_hbm, ti_ref, sems.at[1]),
    ]
    tiles = pltpu.make_async_copy(tiles_hbm, tiles_ref.at[pl.ds(0, slots)], sems.at[2])
    items = pltpu.make_async_copy(item_hbm, item_ref, sems.at[3])
    own = pltpu.make_async_copy(user_hbm, user_ref, sems.at[4])
    for copy in small + [tiles, items, own]:
        copy.start()
    tiles_ref[slots] = jnp.zeros((BLOCK, BLOCK), BF16)
    for block in range(row_blocks * col_blocks):
        head_ref[block] = slots
    next_ref[slots] = -1
    for copy in small:
        copy.wait()

    def place(s, found):
        block = tu_ref[s] * col_blocks + ti_ref[s]
        before = head_ref[block]
        again = next_ref[before] == slots
        next_ref[s] = before
        head_ref[block] = s
        twice_ref[found] = block
        return found + again.astype(jnp.int32)

    found = lax.fori_loop(0, count_ref[0], place, jnp.int32(0))
    tiles.wait()
    for u in range(row_blocks):
        for i in range(col_blocks):
            tile = tiles_ref[head_ref[u * col_blocks + i]]
            r_ref[u * BLOCK : (u + 1) * BLOCK, i * BLOCK : (i + 1) * BLOCK] = tile

    def gather(k, carry):
        block = twice_ref[k]
        start = head_ref[block]
        _, total = lax.while_loop(
            lambda at: at[0] != slots,
            lambda at: (next_ref[at[0]], at[1] + tiles_ref[at[0]].astype(F32)),
            (next_ref[start], tiles_ref[start].astype(F32)),
        )
        rows = pl.ds(pl.multiple_of(block // col_blocks * BLOCK, BLOCK), BLOCK)
        cols = pl.ds(pl.multiple_of(block % col_blocks * BLOCK, BLOCK), BLOCK)
        r_ref[rows, cols] = total.astype(BF16)
        return carry

    lax.fori_loop(0, found, gather, 0)
    items.wait()
    own.wait()
    part = jnp.dot(r_ref[...], item_ref[...], preferred_element_type=F32)
    part_ref[...] = part.astype(BF16)


def first_call(tile_user, tile_item, tile_count, tiles, item_emb, user_emb):
    items, slots = item_emb.shape[0], tiles.shape[0]
    users = user_emb.shape[0]
    blocks = (users // BLOCK) * (items // BLOCK)
    inputs = (tile_user, tile_item, tiles, item_emb, user_emb)
    return pl.pallas_call(
        first_kernel,
        out_shape=(
            jax.ShapeDtypeStruct((users, items), BF16),
            jax.ShapeDtypeStruct((users, DIM), BF16),
            jax.ShapeDtypeStruct((users, DIM), BF16),
        ),
        in_specs=[SMEM] + [HBM] * 5,
        out_specs=(VMEM, VMEM, VMEM),
        scratch_shapes=[
            pltpu.SMEM((slots,), jnp.int32),
            pltpu.SMEM((slots,), jnp.int32),
            pltpu.SMEM((blocks,), jnp.int32),
            pltpu.SMEM((slots + 1,), jnp.int32),
            pltpu.SMEM((slots + 1,), jnp.int32),
            pltpu.VMEM((slots + 1, BLOCK, BLOCK), BF16),
            pltpu.VMEM(item_emb.shape, BF16),
            pltpu.SemaphoreType.DMA((5,)),
        ],
        compiler_params=PARAMS,
        name="first",
    )(tile_count, *(pltpu.with_memory_space_constraint(x, pltpu.HBM) for x in inputs))


def back_kernel(r_ref, user_ref, keep_ref, send_ref, two_ref):
    back = lax.dot_general(r_ref[...], user_ref[...], FIRST_DIMS, preferred_element_type=F32)
    two_ref[...] = back.astype(BF16).reshape(two_ref.shape)
    core = lax.axis_index("core")
    keep_ref[...] = two_ref[core]
    send_ref[...] = two_ref[1 - core]


def back_call(r, user_emb):
    piece = jax.ShapeDtypeStruct((GROUP, r.shape[1] // CORE // GROUP, DIM), BF16)
    return pl.pallas_call(
        back_kernel,
        out_shape=(piece, piece),
        in_specs=[VMEM, VMEM],
        out_specs=(VMEM, VMEM),
        scratch_shapes=[pltpu.VMEM((CORE,) + piece.shape, BF16)],
        compiler_params=PARAMS,
        name="back",
    )(r, user_emb)


def second_kernel(r_ref, parts_ref, one_hbm, keep_ref, send_ref, two_ref, one_ref, sem):
    total = parts_ref[0].astype(F32)
    for k in range(1, parts_ref.shape[0]):
        total += parts_ref[k].astype(F32)
    one = total.astype(BF16)
    one_ref[...] = one
    copy = pltpu.make_async_copy(one_ref, one_hbm, sem)
    copy.start()
    back = lax.dot_general(r_ref[...], one, FIRST_DIMS, preferred_element_type=F32)
    back = back.reshape(ZH, ZL, Y, CORE, 8, DIM)
    for zl in range(ZL):
        for y in range(Y):
            for c in range(CORE):
                rows = jnp.concatenate([back[zh, zl, y, c] for zh in range(ZH)], axis=0)
                two_ref[c, zl * Y + y] = rows.astype(BF16)
    core = lax.axis_index("core")
    keep_ref[...] = two_ref[core]
    send_ref[...] = two_ref[1 - core]
    copy.wait()


def second_call(r, parts):
    users, items = r.shape
    piece = jax.ShapeDtypeStruct((GROUP, items // CORE // GROUP, DIM), BF16)
    return pl.pallas_call(
        second_kernel,
        out_shape=(pltpu.HBM((users, DIM), BF16), piece, piece),
        in_specs=[VMEM, VMEM],
        out_specs=(HBM, VMEM, VMEM),
        scratch_shapes=[
            pltpu.VMEM((CORE,) + piece.shape, BF16),
            pltpu.VMEM((users, DIM), BF16),
            pltpu.SemaphoreType.DMA,
        ],
        compiler_params=PARAMS,
        name="second",
    )(r, parts)


def spread_kernel(got_ref, keep_ref, sent_ref, out_ref):
    total = got_ref[0].astype(F32)
    for k in range(1, got_ref.shape[0]):
        total += got_ref[k].astype(F32)
    total = total.astype(BF16)
    for k in range(out_ref.shape[0]):
        out_ref[k, 0] = total
    other = sent_ref[1 - lax.axis_index("core")].astype(F32)
    out_ref[:, 1] = (keep_ref[...].astype(F32) + other).astype(BF16)


def spread_call(got, keep, sent):
    return pl.pallas_call(
        spread_kernel,
        out_shape=jax.ShapeDtypeStruct((GROUP, 2) + got.shape[1:], BF16),
        in_specs=[VMEM, VMEM, VMEM],
        out_specs=VMEM,
        compiler_params=PARAMS,
        name="spread",
    )(got, keep, sent)


def third_kernel(r_ref, one_ref, emb_ref, part_ref, out_ref):
    part = jnp.dot(r_ref[...], one_ref[...], preferred_element_type=F32)
    part_ref[...] = part.astype(BF16)
    block = (lax.axis_index("zh") * ZL + lax.axis_index("zl")) * Y + lax.axis_index("y")
    rows = pl.ds(pl.multiple_of(block * 16, 16), 16)
    pair = one_ref[rows].astype(F32) + emb_ref[rows].astype(F32)
    mine = jnp.where(lax.axis_index("core") == 0, pair[:8], pair[8:])
    out_ref[...] = mine


def third_call(r, item_one, item_emb):
    users, items = r.shape
    return pl.pallas_call(
        third_kernel,
        out_shape=(
            jax.ShapeDtypeStruct((users, DIM), BF16),
            jax.ShapeDtypeStruct((8, DIM), F32),
        ),
        in_specs=[VMEM, VMEM, VMEM],
        out_specs=(VMEM, VMEM),
        compiler_params=PARAMS,
        name="third",
    )(r, item_one, item_emb)


def last_kernel(user_ref, one_ref, parts_ref, base_ref, two_ref, user_out_ref, item_out_ref):
    total = user_ref[...].astype(F32) + one_ref[...].astype(F32)
    for k in range(parts_ref.shape[0]):
        total += parts_ref[k].astype(F32)
    user_out_ref[...] = (total / 3.0).astype(BF16)
    two = two_ref[...].astype(F32).sum(axis=0)
    item_out_ref[...] = ((base_ref[...] + two) / 3.0).astype(BF16)


def last_call(user_emb, user_one, parts, base, two):
    return pl.pallas_call(
        last_kernel,
        out_shape=(
            jax.ShapeDtypeStruct(user_emb.shape, BF16),
            jax.ShapeDtypeStruct(base.shape, BF16),
        ),
        in_specs=[VMEM] * 5,
        out_specs=(VMEM, VMEM),
        compiler_params=PARAMS,
        name="last",
    )(user_emb, user_one, parts, base, two)


def swap(x, axis):
    return lax.all_to_all(x, axis, 0, 0, tiled=True)


def add_up(x):
    return x.astype(F32).sum(axis=0)


def per_device(tiles, tile_user, tile_item, tile_count, user_emb, item_emb):
    r, part, own = first_call(tile_user, tile_item, tile_count, tiles, item_emb, user_emb)
    keep, send = back_call(r, own)
    other = lax.ppermute(send, "core", [(0, 1), (1, 0)])
    chip = (keep.astype(F32) + other.astype(F32)).astype(BF16)
    chip, part = lax.optimization_barrier((chip, part))
    got = swap(chip, ("zl", "y"))
    parts = lax.all_gather(part, "item", axis=0)

    got, parts = lax.optimization_barrier((got, parts))
    rows = add_up(got).astype(BF16)
    wide = jnp.broadcast_to(rows[None], (ZH,) + rows.shape)
    wide, parts = lax.optimization_barrier((wide, parts))
    got = swap(wide, "zh")
    user_one, keep, send = second_call(r, parts)
    sent = lax.all_gather(send, "core", axis=0)
    got = swap(spread_call(got, keep, sent), ("zl", "y"))

    two = add_up(got[:, 1]).astype(BF16)
    half, two = lax.optimization_barrier((got[:, 0], two))
    two = swap(two.reshape(ZH, -1, DIM), "zh")
    item_one = lax.all_gather(half.reshape(-1, DIM), "core", axis=0, tiled=True)
    part, base = third_call(r, item_one, item_emb)
    parts = lax.all_gather(part, "item", axis=0)
    return last_call(user_emb, user_one, parts, base, two)


def solution(mesh):
    fine = Mesh(mesh.devices.reshape(ZH, ZL, Y, CORE, -1), AXES + ("item",))
    every = P(AXES + ("item",))
    in_specs = (every, every, every, every, P(AXES, None), P("item", None))
    out_specs = (P(AXES, None), P(("item",) + AXES, None))
    return jax.shard_map(
        per_device, mesh=fine, in_specs=in_specs, out_specs=out_specs, check_vma=False
    )
```

time: 113 us -> 108 us (0.956)
  blocking collectives: 102 us -> 53.3 us
  starting transfers between devices: 1.92 us -> 30.8 us
  waiting for transfers between devices: 1.88 us -> 13.3 us
    all_to_all x3 -> x1, blocking collectives: 72.3 us -> 18.3 us  [swap(): return lax.all_to_all(x, axis, 0, 0, tiled=True)]
    all_to_all x0 -> x3, starting transfers between devices: none -> 28.9 us  [swap(): return lax.all_to_all(x, axis, 0, 0, tiled=True)]
    all_gather x1 -> x2, blocking collectives: 13.4 us -> 30.7 us  [per_device(): parts = lax.all_gather(part, 'item', axis=0)]
    all_to_all x0 -> x3, waiting for transfers between devices: none -> 11.8 us  [swap(): return lax.all_to_all(x, axis, 0, 0, tiled=True)]
    all_gather x1, blocking collectives: 13.7 us -> 2.18 us  [per_device(): sent = lax.all_gather(send, 'core', axis=0)]
    pallas_call x2 -> x4, Pallas kernels: 1.16 us -> 2.73 us  [the longest x1 0.97 us: second_call(): pl.pallas_call(second_kernel, out_shape=(pltpu.HBM((users, DIM), BF16), p...]
  transfers between devices with their start and end apart: 1 -> 4, of which waited for: 1 -> 2; matrix products, arithmetic and copies ran while one was open for 0% -> 0% of each run, Pallas kernels for 0% -> 2%
where the time goes in v3:
time: 108 us; the launch traced here: 107 us
  blocking collectives  53.3 us (49%)
  starting transfers between devices  30.8 us (29%)
  waiting for transfers between devices  13.3 us (12%)
  Pallas kernels  6.15 us (6%)
  other arithmetic  1.46 us (1%)
  between operations  1.33 us (1%)
    all_gather x2, blocking collectives, per_device(): parts = lax.all_gather(part, 'item', axis=0)  30.7 us
    all_to_all x3, starting transfers between devices, swap(): return lax.all_to_all(x, axis, 0, 0, tiled=True)  28.9 us
    all_to_all x1, blocking collectives, swap(): return lax.all_to_all(x, axis, 0, 0, tiled=True)  18.3 us
    all_to_all x3, waiting for transfers between devices, swap(): return lax.all_to_all(x, axis, 0, 0, tiled=True)  11.8 us
    pallas_call x1, Pallas kernels, first_call(): pl.pallas_call(first_kernel, out_shape=(jax.ShapeDtypeStruct((users, item...  2.71 us
    all_gather x1, blocking collectives, per_device(): sent = lax.all_gather(send, 'core', axis=0)  2.18 us
    all_gather x1, blocking collectives, per_device(): item_one = lax.all_gather(half.reshape(-1, DIM), 'core', axis=0, tiled=True)  2.17 us
  transfers between devices with their start and end apart: 4, of which 2 were waited for; matrix products, arithmetic and copies ran while one was open for 0% of the time, Pallas kernels for 2%

profile of v3, /device:TPU:10, one launch (start us, length us, event | category | flops | bytes accessed | tf_op | source)
XLA Modules:
  0.0 107.0 jit_solution(12733740925997627959)
XLA Ops:
  1.3 2.7 %first.1 = (bf16[512,2048]{1,0:T(8,128)(2,1)S(1)}, bf16[512,128]{1,0:T(8,128)(2,1)S(1)}, bf16[512,128]{1,0:T(8,128)(2,1)S(1)}) custom-call(s32[1]{0:T(128)S(6)} %copy.8.count_ref, s32[48]{0:T(128)} %tu_hbm.1, s32[48]{0:T(128)} %ti_hbm.1, bf16[48,128,128]{2,1,0:T(8,128)(2,1)} %tiles_hbm.1, bf16[2048,128]{1,0:T(8,128)(2,1)} %emb_ref.1, bf16[512,128]{1,0:T(8,128)(2,1)} %user_ref.1), custom_call_target="tpu_custom_call" | custom-call | tf_op jit(solution)/shard_map/first/pallas_call | solution.py:86
  4.0 0.9 back.1
  4.9 1.9 %collective-permute-start = (bf16[16,64,128]{2,1,0:T(8,128)(2,1)S(1)}, bf16[16,64,128]{2,1,0:T(8,128)(2,1)S(1)}, u32[]{:S(2)}, u32[]{:S(2)}) collective-permute-start(bf16[16,64,128]{2,1,0:T(8,128)(2,1)S(1)} %get-tuple-element.23), channel_id=1, source_target_pairs={{0,4},{4,0},{1,5},{5,1},{2,6},{6,2},{3,7},{7,3},{8,12},{12,8},{9,1... | collective-permute-start | bytes 786440 | tf_op jit(solution)/shard_map/ppermute | solution.py:251
  6.8 1.5 %collective-permute-done = bf16[16,64,128]{2,1,0:T(8,128)(2,1)S(1)} collective-permute-done((bf16[16,64,128]{2,1,0:T(8,128)(2,1)S(1)}, bf16[16,64,128]{2,1,0:T(8,128)(2,1)S(1)}, u32[]{:S(2)}, u32[]{:S(2)}) %collective-permute-start) | collective-permute-done | bytes 262176 | tf_op jit(solution)/shard_map/ppermute | solution.py:251
  8.3 0.8 add_convert_fusion
  9.1 9.5 %all-to-all-start = ((bf16[16,64,128]{2,1,0:T(8,128)(2,1)}), bf16[16,64,128]{2,1,0:T(8,128)(2,1)S(1)}, u32[]{:S(2)}, u32[]{:S(2)}) async-start(bf16[16,64,128]{2,1,0:T(8,128)(2,1)} %add_convert_fusion), calls=%async_computation | async-start | bytes 524288 | tf_op jit(solution)/shard_map/all_to_all | solution.py:241
  18.7 17.3 %all-gather = bf16[2048,128]{1,0:T(8,128)(2,1)S(1)} all-gather(bf16[512,128]{1,0:T(8,128)(2,1)S(1)} %get-tuple-element.26), channel_id=2, replica_groups=mesh['zh'=8,'zl'=2,'y'=8,'core'=2,'item'=4] {'item'}, dimensions={0}, use_global_device_ids=true | all-gather | bytes 655360 | tf_op jit(solution)/shard_map/all_gather | solution.py:255
  36.0 0.0 all-to-all-done
  36.0 0.7 broadcast_in_dim.2
  36.7 14.1 %all-to-all-start.1 = ((bf16[8,64,128]{2,1,0:T(8,128)(2,1)}), bf16[8,64,128]{2,1,0:T(8,128)(2,1)S(1)}, u32[]{:S(2)}, u32[]{:S(2)}) async-start(bf16[8,64,128]{2,1,0:T(8,128)(2,1)} %broadcast_in_dim.2), calls=%async_computation.1 | async-start | bytes 262144 | tf_op jit(solution)/shard_map/all_to_all | solution.py:241
  50.7 1.0 second.1
  51.7 2.2 %all-gather.1 = bf16[32,64,128]{2,1,0:T(8,128)(2,1)S(1)} all-gather(bf16[16,64,128]{2,1,0:T(8,128)(2,1)S(1)} %get-tuple-element.33), channel_id=3, replica_groups=mesh['zh'=8,'zl'=2,'y'=8,'core'=2,'item'=4] {'core'}, dimensions={0}, use_global_device_ids=true | all-gather | bytes 786432 | tf_op jit(solution)/shard_map/all_gather | solution.py:263
  53.9 0.0 copy-start
  53.9 11.8 %all-to-all-done.1.got_ref = bf16[8,64,128]{2,1,0:T(8,128)(2,1)S(1)} async-done(((bf16[8,64,128]{2,1,0:T(8,128)(2,1)}), bf16[8,64,128]{2,1,0:T(8,128)(2,1)S(1)}, u32[]{:S(2)}, u32[]{:S(2)}) %all-to-all-start.1) | async-done | bytes 131104 | tf_op jit(solution)/shard_map/all_to_all | solution.py:241
  65.7 0.1 spread.1
  65.8 18.3 %all_to_all.20 = bf16[16,2,64,128]{3,2,1,0:T(8,128)(2,1)S(1)} all-to-all(bf16[16,2,64,128]{3,2,1,0:T(8,128)(2,1)S(1)} %spread.1), channel_id=1, replica_groups=mesh['zh'=8,'zl'=2,'y'=8,'core'=2,'item'=4] {'zl','y'}, dimensions={0} | all-to-all | bytes 1048576 | tf_op jit(solution)/shard_map/all_to_all | solution.py:241
  84.1 0.6 slice_reduce_fusion
  84.7 5.3 %all-to-all-start.3 = ((bf16[8,8,128]{2,1,0:T(8,128)(2,1)}), bf16[8,8,128]{2,1,0:T(8,128)(2,1)S(1)}, u32[]{:S(2)}, u32[]{:S(2)}) async-start(bf16[8,8,128]{2,1,0:T(8,128)(2,1)} %bitcast.5), calls=%async_computation.3 | async-start | bytes 32768 | tf_op jit(solution)/shard_map/all_to_all | solution.py:241
  90.0 2.2 %all_gather.25.one_ref = bf16[2048,128]{1,0:T(8,128)(2,1)S(1)} all-gather(bf16[1024,128]{1,0:T(8,128)(2,1)S(1)} %bitcast.10), channel_id=1, replica_groups=mesh['zh'=8,'zl'=2,'y'=8,'core'=2,'item'=4] {'core'}, dimensions={0}, use_global_device_ids=true | all-gather | bytes 786432 | tf_op jit(solution)/shard_map/all_gather | solution.py:269
  92.2 0.0 copy-done
  92.2 0.0 copy-start.1
  92.2 0.0 copy-start.2
  92.2 0.7 third.1
  92.9 13.4 %all-gather.2 = bf16[2048,128]{1,0:T(8,128)(2,1)S(1)} all-gather(bf16[512,128]{1,0:T(8,128)(2,1)S(1)} %get-tuple-element.35), channel_id=4, replica_groups=mesh['zh'=8,'zl'=2,'y'=8,'core'=2,'item'=4] {'item'}, dimensions={0}, use_global_device_ids=true | all-gather | bytes 655360 | tf_op jit(solution)/shard_map/all_gather | solution.py:271
  106.3 0.0 all-to-all-done.3.two_ref
  106.3 0.0 copy-done.1
  106.3 0.0 copy-done.2
  106.3 0.8 last.1
  (1 shorter events, 0.0 us)
Async XLA Ops:
  4.9 3.4 %collective-permute-start = (bf16[16,64,128]{2,1,0:T(8,128)(2,1)S(1)}, bf16[16,64,128]{2,1,0:T(8,128)(2,1)S(1)}, u32[]{:S(2)}, u32[]{:S(2)}) collective-permute-start(bf16[16,64,128]{2,1,0:T(8,128)(2,1)S(1)} %get-tuple-element.23), channel_id=1, source_target_pairs={{0,4},{4,0},{1,5},{5,1},{2,6},{6,2},{3,7},{7,3},{8,12},{12,8},{9,1... | collective-permute-start | bytes 786440 | tf_op jit(solution)/shard_map/ppermute | solution.py:251
  9.1 26.9 %all-to-all-start = ((bf16[16,64,128]{2,1,0:T(8,128)(2,1)}), bf16[16,64,128]{2,1,0:T(8,128)(2,1)S(1)}, u32[]{:S(2)}, u32[]{:S(2)}) async-start(bf16[16,64,128]{2,1,0:T(8,128)(2,1)} %add_convert_fusion), calls=%async_computation | async-start | bytes 524288 | tf_op jit(solution)/shard_map/all_to_all | solution.py:241
  36.7 29.0 %all-to-all-start.1 = ((bf16[8,64,128]{2,1,0:T(8,128)(2,1)}), bf16[8,64,128]{2,1,0:T(8,128)(2,1)S(1)}, u32[]{:S(2)}, u32[]{:S(2)}) async-start(bf16[8,64,128]{2,1,0:T(8,128)(2,1)} %broadcast_in_dim.2), calls=%async_computation.1 | async-start | bytes 262144 | tf_op jit(solution)/shard_map/all_to_all | solution.py:241
  53.9 38.3 %copy-start = (bf16[2048,128]{1,0:T(8,128)(2,1)S(1)}, bf16[2048,128]{1,0:T(8,128)(2,1)}, u32[]{:S(2)}) copy-start(bf16[2048,128]{1,0:T(8,128)(2,1)} %emb_ref.1) | copy-start | bytes 1572868
  84.7 21.5 %all-to-all-start.3 = ((bf16[8,8,128]{2,1,0:T(8,128)(2,1)}), bf16[8,8,128]{2,1,0:T(8,128)(2,1)S(1)}, u32[]{:S(2)}, u32[]{:S(2)}) async-start(bf16[8,8,128]{2,1,0:T(8,128)(2,1)} %bitcast.5), calls=%async_computation.3 | async-start | bytes 32768 | tf_op jit(solution)/shard_map/all_to_all | solution.py:241
  92.2 14.1 %copy-start.1 = (bf16[512,128]{1,0:T(8,128)(2,1)S(1)}, bf16[512,128]{1,0:T(8,128)(2,1)}, u32[]{:S(2)}) copy-start(bf16[512,128]{1,0:T(8,128)(2,1)} %user_ref.1) | copy-start | bytes 393220
  92.2 14.1 %copy-start.2 = (bf16[512,128]{1,0:T(8,128)(2,1)S(1)}, bf16[512,128]{1,0:T(8,128)(2,1)}, u32[]{:S(2)}) copy-start(bf16[512,128]{1,0:T(8,128)(2,1)} %get-tuple-element.30.one_ref) | copy-start | bytes 393220

commit v4 on v3

--- a/solution.py
+++ b/solution.py
@@ -21,9 +21,9 @@
 FIRST_DIMS = (((0,), (0,)), ((), ()))
 
 
-def first_kernel(count_ref, tu_hbm, ti_hbm, tiles_hbm, item_hbm, user_hbm, r_ref, part_ref, user_ref,
+def first_kernel(count_ref, tu_hbm, ti_hbm, tiles_hbm, item_hbm, user_hbm, r_ref, item_ref, user_ref,
                  tu_ref, ti_ref, head_ref, next_ref, twice_ref,
-                 tiles_ref, item_ref, sems):
+                 tiles_ref, sems):
     slots = tiles_hbm.shape[0]
     row_blocks, col_blocks = r_ref.shape[0] // BLOCK, r_ref.shape[1] // BLOCK
     small = [
@@ -74,8 +74,6 @@
     lax.fori_loop(0, found, gather, 0)
     items.wait()
     own.wait()
-    part = jnp.dot(r_ref[...], item_ref[...], preferred_element_type=F32)
-    part_ref[...] = part.astype(BF16)
 
 
 def first_call(tile_user, tile_item, tile_count, tiles, item_emb, user_emb):
@@ -87,7 +85,7 @@
         first_kernel,
         out_shape=(
             jax.ShapeDtypeStruct((users, items), BF16),
-            jax.ShapeDtypeStruct((users, DIM), BF16),
+            jax.ShapeDtypeStruct((items, DIM), BF16),
             jax.ShapeDtypeStruct((users, DIM), BF16),
         ),
         in_specs=[SMEM] + [HBM] * 5,
@@ -99,12 +97,27 @@
             pltpu.SMEM((slots + 1,), jnp.int32),
             pltpu.SMEM((slots + 1,), jnp.int32),
             pltpu.VMEM((slots + 1, BLOCK, BLOCK), BF16),
-            pltpu.VMEM(item_emb.shape, BF16),
             pltpu.SemaphoreType.DMA((5,)),
         ],
         compiler_params=PARAMS,
         name="first",
     )(tile_count, *(pltpu.with_memory_space_constraint(x, pltpu.HBM) for x in inputs))
+
+
+def part_kernel(r_ref, item_ref, part_ref):
+    part = jnp.dot(r_ref[...], item_ref[...], preferred_element_type=F32)
+    part_ref[...] = part.astype(BF16)
+
+
+def part_call(r, item_emb):
+    return pl.pallas_call(
+        part_kernel,
+        out_shape=jax.ShapeDtypeStruct((r.shape[0], DIM), BF16),
+        in_specs=[VMEM, VMEM],
+        out_specs=VMEM,
+        compiler_params=PARAMS,
+        name="part",
+    )(r, item_emb)
 
 
 def back_kernel(r_ref, user_ref, keep_ref, send_ref, two_ref):
@@ -246,8 +259,10 @@
 
 
 def per_device(tiles, tile_user, tile_item, tile_count, user_emb, item_emb):
-    r, part, own = first_call(tile_user, tile_item, tile_count, tiles, item_emb, user_emb)
+    r, items, own = first_call(tile_user, tile_item, tile_count, tiles, item_emb, user_emb)
     keep, send = back_call(r, own)
+    items, send = lax.optimization_barrier((items, send))
+    part = part_call(r, items)
     other = lax.ppermute(send, "core", [(0, 1), (1, 0)])
     chip = (keep.astype(F32) + other.astype(F32)).astype(BF16)
     chip, part = lax.optimization_barrier((chip, part))
@@ -264,10 +279,11 @@
     got = swap(spread_call(got, keep, sent), ("zl", "y"))
 
     two = add_up(got[:, 1]).astype(BF16)
-    half, two = lax.optimization_barrier((got[:, 0], two))
-    two = swap(two.reshape(ZH, -1, DIM), "zh")
+    half = got[:, 0]
     item_one = lax.all_gather(half.reshape(-1, DIM), "core", axis=0, tiled=True)
     part, base = third_call(r, item_one, item_emb)
+    two, part = lax.optimization_barrier((two, part))
+    two = swap(two.reshape(ZH, -1, DIM), "zh")
     parts = lax.all_gather(part, "item", axis=0)
     return last_call(user_emb, user_one, parts, base, two)
 

time: 108 us -> 107 us (level)
  no operation moved by 1% of the time
where the time goes in v4:
time: 107 us; the launch traced here: 106 us
  blocking collectives  53.7 us (50%)
  starting transfers between devices  30.4 us (28%)
  waiting for transfers between devices  12.6 us (12%)
  Pallas kernels  6.21 us (6%)
  other arithmetic  1.46 us (1%)
  between operations  1.33 us (1%)
    all_gather x2, blocking collectives, per_device(): parts = lax.all_gather(part, 'item', axis=0)  31 us
    all_to_all x3, starting transfers between devices, swap(): return lax.all_to_all(x, axis, 0, 0, tiled=True)  28.5 us
    all_to_all x1, blocking collectives, swap(): return lax.all_to_all(x, axis, 0, 0, tiled=True)  18.3 us
    all_to_all x3, waiting for transfers between devices, swap(): return lax.all_to_all(x, axis, 0, 0, tiled=True)  11.8 us
    all_gather x1, blocking collectives, per_device(): sent = lax.all_gather(send, 'core', axis=0)  2.18 us
    all_gather x1, blocking collectives, per_device(): item_one = lax.all_gather(half.reshape(-1, DIM), 'core', axis=0, tiled=True)  2.17 us
  transfers between devices with their start and end apart: 4, of which 2 were waited for; matrix products, arithmetic and copies ran while one was open for 0% of the time, Pallas kernels for 2%

profile of v4, /device:TPU:10, one launch (start us, length us, event | category | flops | bytes accessed | tf_op | source)
XLA Modules:
  0.0 106.3 jit_solution(14177194632482332163)
XLA Ops:
  1.3 2.1 %first.1 = (bf16[512,2048]{1,0:T(8,128)(2,1)S(1)}, bf16[2048,128]{1,0:T(8,128)(2,1)S(1)}, bf16[512,128]{1,0:T(8,128)(2,1)S(1)}) custom-call(s32[1]{0:T(128)S(6)} %copy.8.count_ref, s32[48]{0:T(128)} %tu_hbm.1, s32[48]{0:T(128)} %ti_hbm.1, bf16[48,128,128]{2,1,0:T(8,128)(2,1)} %tiles_hbm.1, bf16[2048,128]{1,0:T(8,128)(2,1)} %emb_ref.1, bf16[512,128]{1,0:T(8,128)(2,1)} %user_ref.1), custom_call_target="tpu_custom_call" | custom-call | tf_op jit(solution)/shard_map/first/pallas_call | solution.py:84
  3.3 0.9 back.1
  4.3 1.9 %collective-permute-start = (bf16[16,64,128]{2,1,0:T(8,128)(2,1)S(1)}, bf16[16,64,128]{2,1,0:T(8,128)(2,1)S(1)}, u32[]{:S(2)}, u32[]{:S(2)}) collective-permute-start(bf16[16,64,128]{2,1,0:T(8,128)(2,1)S(1)} %get-tuple-element.27), channel_id=1, source_target_pairs={{0,4},{4,0},{1,5},{5,1},{2,6},{6,2},{3,7},{7,3},{8,12},{12,8},{9,1... | collective-permute-start | bytes 786440 | tf_op jit(solution)/shard_map/ppermute | solution.py:266
  6.2 0.7 part.1
  6.9 0.8 collective-permute-done
  7.7 0.8 add_convert_fusion
  8.5 9.3 %all-to-all-start = ((bf16[16,64,128]{2,1,0:T(8,128)(2,1)}), bf16[16,64,128]{2,1,0:T(8,128)(2,1)S(1)}, u32[]{:S(2)}, u32[]{:S(2)}) async-start(bf16[16,64,128]{2,1,0:T(8,128)(2,1)} %add_convert_fusion), calls=%async_computation | async-start | bytes 524288 | tf_op jit(solution)/shard_map/all_to_all | solution.py:254
  17.8 17.6 %all-gather = bf16[2048,128]{1,0:T(8,128)(2,1)S(1)} all-gather(bf16[512,128]{1,0:T(8,128)(2,1)S(1)} %part.1), channel_id=2, replica_groups=mesh['zh'=8,'zl'=2,'y'=8,'core'=2,'item'=4] {'item'}, dimensions={0}, use_global_device_ids=true | all-gather | bytes 655360 | tf_op jit(solution)/shard_map/all_gather | solution.py:270
  35.3 0.0 all-to-all-done
  35.4 0.7 broadcast_in_dim.2
  36.1 13.9 %all-to-all-start.1 = ((bf16[8,64,128]{2,1,0:T(8,128)(2,1)}), bf16[8,64,128]{2,1,0:T(8,128)(2,1)S(1)}, u32[]{:S(2)}, u32[]{:S(2)}) async-start(bf16[8,64,128]{2,1,0:T(8,128)(2,1)} %broadcast_in_dim.2), calls=%async_computation.1 | async-start | bytes 262144 | tf_op jit(solution)/shard_map/all_to_all | solution.py:254
  50.0 1.0 second.1
  50.9 2.2 %all-gather.1 = bf16[32,64,128]{2,1,0:T(8,128)(2,1)S(1)} all-gather(bf16[16,64,128]{2,1,0:T(8,128)(2,1)S(1)} %get-tuple-element.37), channel_id=3, replica_groups=mesh['zh'=8,'zl'=2,'y'=8,'core'=2,'item'=4] {'core'}, dimensions={0}, use_global_device_ids=true | all-gather | bytes 786432 | tf_op jit(solution)/shard_map/all_gather | solution.py:278
  53.1 0.0 copy-start
  53.1 11.8 %all-to-all-done.1.got_ref = bf16[8,64,128]{2,1,0:T(8,128)(2,1)S(1)} async-done(((bf16[8,64,128]{2,1,0:T(8,128)(2,1)}), bf16[8,64,128]{2,1,0:T(8,128)(2,1)S(1)}, u32[]{:S(2)}, u32[]{:S(2)}) %all-to-all-start.1) | async-done | bytes 131104 | tf_op jit(solution)/shard_map/all_to_all | solution.py:254
  64.9 0.1 spread.1
  65.0 18.3 %all_to_all.20 = bf16[16,2,64,128]{3,2,1,0:T(8,128)(2,1)S(1)} all-to-all(bf16[16,2,64,128]{3,2,1,0:T(8,128)(2,1)S(1)} %spread.1), channel_id=1, replica_groups=mesh['zh'=8,'zl'=2,'y'=8,'core'=2,'item'=4] {'zl','y'}, dimensions={0} | all-to-all | bytes 1048576 | tf_op jit(solution)/shard_map/all_to_all | solution.py:254
  83.3 0.6 fusion
  84.0 2.2 %all_gather.25.one_ref = bf16[2048,128]{1,0:T(8,128)(2,1)S(1)} all-gather(bf16[1024,128]{1,0:T(8,128)(2,1)S(1)} %bitcast.8), channel_id=1, replica_groups=mesh['zh'=8,'zl'=2,'y'=8,'core'=2,'item'=4] {'core'}, dimensions={0}, use_global_device_ids=true | all-gather | bytes 786432 | tf_op jit(solution)/shard_map/all_gather | solution.py:283
  86.1 0.0 copy-done
  86.1 0.0 copy-start.1
  86.1 0.0 copy-start.2
  86.1 0.7 third.1
  86.9 5.3 %all-to-all-start.3 = ((bf16[8,8,128]{2,1,0:T(8,128)(2,1)}), bf16[8,8,128]{2,1,0:T(8,128)(2,1)S(1)}, u32[]{:S(2)}, u32[]{:S(2)}) async-start(bf16[8,8,128]{2,1,0:T(8,128)(2,1)} %bitcast.4), calls=%async_computation.3 | async-start | bytes 32768 | tf_op jit(solution)/shard_map/all_to_all | solution.py:254
  92.1 13.4 %all-gather.2 = bf16[2048,128]{1,0:T(8,128)(2,1)S(1)} all-gather(bf16[512,128]{1,0:T(8,128)(2,1)S(1)} %get-tuple-element.39), channel_id=4, replica_groups=mesh['zh'=8,'zl'=2,'y'=8,'core'=2,'item'=4] {'item'}, dimensions={0}, use_global_device_ids=true | all-gather | bytes 655360 | tf_op jit(solution)/shard_map/all_gather | solution.py:287
  105.6 0.0 all-to-all-done.3.two_ref
  105.6 0.0 copy-done.1
  105.6 0.0 copy-done.2
  105.6 0.8 last.1
  (1 shorter events, 0.0 us)
Async XLA Ops:
  4.3 3.4 %collective-permute-start = (bf16[16,64,128]{2,1,0:T(8,128)(2,1)S(1)}, bf16[16,64,128]{2,1,0:T(8,128)(2,1)S(1)}, u32[]{:S(2)}, u32[]{:S(2)}) collective-permute-start(bf16[16,64,128]{2,1,0:T(8,128)(2,1)S(1)} %get-tuple-element.27), channel_id=1, source_target_pairs={{0,4},{4,0},{1,5},{5,1},{2,6},{6,2},{3,7},{7,3},{8,12},{12,8},{9,1... | collective-permute-start | bytes 786440 | tf_op jit(solution)/shard_map/ppermute | solution.py:266
  8.5 26.9 %all-to-all-start = ((bf16[16,64,128]{2,1,0:T(8,128)(2,1)}), bf16[16,64,128]{2,1,0:T(8,128)(2,1)S(1)}, u32[]{:S(2)}, u32[]{:S(2)}) async-start(bf16[16,64,128]{2,1,0:T(8,128)(2,1)} %add_convert_fusion), calls=%async_computation | async-start | bytes 524288 | tf_op jit(solution)/shard_map/all_to_all | solution.py:254
  36.1 28.8 %all-to-all-start.1 = ((bf16[8,64,128]{2,1,0:T(8,128)(2,1)}), bf16[8,64,128]{2,1,0:T(8,128)(2,1)S(1)}, u32[]{:S(2)}, u32[]{:S(2)}) async-start(bf16[8,64,128]{2,1,0:T(8,128)(2,1)} %broadcast_in_dim.2), calls=%async_computation.1 | async-start | bytes 262144 | tf_op jit(solution)/shard_map/all_to_all | solution.py:254
  53.1 33.0 %copy-start = (bf16[2048,128]{1,0:T(8,128)(2,1)S(1)}, bf16[2048,128]{1,0:T(8,128)(2,1)}, u32[]{:S(2)}) copy-start(bf16[2048,128]{1,0:T(8,128)(2,1)} %emb_ref.1) | copy-start | bytes 1572868
  86.1 19.4 %copy-start.1 = (bf16[512,128]{1,0:T(8,128)(2,1)S(1)}, bf16[512,128]{1,0:T(8,128)(2,1)}, u32[]{:S(2)}) copy-start(bf16[512,128]{1,0:T(8,128)(2,1)} %user_ref.1) | copy-start | bytes 393220
  86.1 19.4 %copy-start.2 = (bf16[512,128]{1,0:T(8,128)(2,1)S(1)}, bf16[512,128]{1,0:T(8,128)(2,1)}, u32[]{:S(2)}) copy-start(bf16[512,128]{1,0:T(8,128)(2,1)} %get-tuple-element.34.one_ref) | copy-start | bytes 393220
  86.9 18.7 %all-to-all-start.3 = ((bf16[8,8,128]{2,1,0:T(8,128)(2,1)}), bf16[8,8,128]{2,1,0:T(8,128)(2,1)S(1)}, u32[]{:S(2)}, u32[]{:S(2)}) async-start(bf16[8,8,128]{2,1,0:T(8,128)(2,1)} %bitcast.4), calls=%async_computation.3 | async-start | bytes 32768 | tf_op jit(solution)/shard_map/all_to_all | solution.py:254

commit v5 on v4

--- a/solution.py
+++ b/solution.py
@@ -141,6 +141,22 @@
     )(r, user_emb)
 
 
+def join_kernel(keep_ref, sent_ref, out_ref):
+    other = sent_ref[1 - lax.axis_index("core")].astype(F32)
+    out_ref[...] = (keep_ref[...].astype(F32) + other).astype(BF16)
+
+
+def join_call(keep, sent):
+    return pl.pallas_call(
+        join_kernel,
+        out_shape=jax.ShapeDtypeStruct(keep.shape, BF16),
+        in_specs=[VMEM, VMEM],
+        out_specs=VMEM,
+        compiler_params=PARAMS,
+        name="join",
+    )(keep, sent)
+
+
 def second_kernel(r_ref, parts_ref, one_hbm, keep_ref, send_ref, two_ref, one_ref, sem):
     total = parts_ref[0].astype(F32)
     for k in range(1, parts_ref.shape[0]):
@@ -202,9 +218,10 @@
     )(got, keep, sent)
 
 
-def third_kernel(r_ref, one_ref, emb_ref, part_ref, out_ref):
+def third_kernel(r_ref, one_ref, emb_ref, back_ref, part_ref, out_ref, two_ref):
     part = jnp.dot(r_ref[...], one_ref[...], preferred_element_type=F32)
     part_ref[...] = part.astype(BF16)
+    two_ref[...] = back_ref[...].astype(F32).sum(axis=0).astype(BF16)
     block = (lax.axis_index("zh") * ZL + lax.axis_index("zl")) * Y + lax.axis_index("y")
     rows = pl.ds(pl.multiple_of(block * 16, 16), 16)
     pair = one_ref[rows].astype(F32) + emb_ref[rows].astype(F32)
@@ -212,19 +229,20 @@
     out_ref[...] = mine
 
 
-def third_call(r, item_one, item_emb):
+def third_call(r, item_one, item_emb, back):
     users, items = r.shape
     return pl.pallas_call(
         third_kernel,
         out_shape=(
             jax.ShapeDtypeStruct((users, DIM), BF16),
             jax.ShapeDtypeStruct((8, DIM), F32),
+            jax.ShapeDtypeStruct(back.shape[1:], BF16),
         ),
-        in_specs=[VMEM, VMEM, VMEM],
-        out_specs=(VMEM, VMEM),
+        in_specs=[VMEM] * 4,
+        out_specs=(VMEM, VMEM, VMEM),
         compiler_params=PARAMS,
         name="third",
-    )(r, item_one, item_emb)
+    )(r, item_one, item_emb, back)
 
 
 def last_kernel(user_ref, one_ref, parts_ref, base_ref, two_ref, user_out_ref, item_out_ref):
@@ -261,28 +279,26 @@
 def per_device(tiles, tile_user, tile_item, tile_count, user_emb, item_emb):
     r, items, own = first_call(tile_user, tile_item, tile_count, tiles, item_emb, user_emb)
     keep, send = back_call(r, own)
-    items, send = lax.optimization_barrier((items, send))
+    chip = join_call(keep, lax.all_gather(send, "core", axis=0))
+    chip, items = lax.optimization_barrier((chip, items))
+    got = swap(chip, ("zl", "y"))
     part = part_call(r, items)
-    other = lax.ppermute(send, "core", [(0, 1), (1, 0)])
-    chip = (keep.astype(F32) + other.astype(F32)).astype(BF16)
-    chip, part = lax.optimization_barrier((chip, part))
-    got = swap(chip, ("zl", "y"))
-    parts = lax.all_gather(part, "item", axis=0)
-
-    got, parts = lax.optimization_barrier((got, parts))
+    near = lax.all_gather(part, "item", axis=0, axis_index_groups=[[0, 1], [2, 3]])
+    pair = add_up(near).astype(BF16)
+
+    got, pair = lax.optimization_barrier((got, pair))
     rows = add_up(got).astype(BF16)
     wide = jnp.broadcast_to(rows[None], (ZH,) + rows.shape)
-    wide, parts = lax.optimization_barrier((wide, parts))
+    wide, pair = lax.optimization_barrier((wide, pair))
     got = swap(wide, "zh")
+    parts = lax.all_gather(pair, "item", axis=0, axis_index_groups=[[0, 3], [1, 2]])
     user_one, keep, send = second_call(r, parts)
     sent = lax.all_gather(send, "core", axis=0)
     got = swap(spread_call(got, keep, sent), ("zl", "y"))
 
-    two = add_up(got[:, 1]).astype(BF16)
-    half = got[:, 0]
+    half, back = got[:, 0], got[:, 1]
     item_one = lax.all_gather(half.reshape(-1, DIM), "core", axis=0, tiled=True)
-    part, base = third_call(r, item_one, item_emb)
-    two, part = lax.optimization_barrier((two, part))
+    part, base, two = third_call(r, item_one, item_emb, back)
     two = swap(two.reshape(ZH, -1, DIM), "zh")
     parts = lax.all_gather(part, "item", axis=0)
     return last_call(user_emb, user_one, parts, base, two)

time: 107 us -> 106 us (level)
  waiting for transfers between devices: 12.6 us -> 6.51 us
  starting transfers between devices: 30.4 us -> 33.4 us
  blocking collectives: 53.7 us -> 56.2 us
  other arithmetic: 1.46 us -> 0.09 us
  Pallas kernels: 6.21 us -> 7.48 us
    all_gather x0 -> x3, blocking collectives: none -> 19.2 us  [the longest x1 11.4 us: per_device(): lax.all_gather(part, 'item', axis=0, axis_index_groups=[[0, 1], [2, 3]])]
    all_gather x2 -> x1, blocking collectives: 31 us -> 14.9 us  [per_device(): parts = lax.all_gather(part, 'item', axis=0)]
    all_to_all x3, waiting for transfers between devices: 11.8 us -> 6.51 us  [swap(): return lax.all_to_all(x, axis, 0, 0, tiled=True)]
    all_to_all x3, starting transfers between devices: 28.5 us -> 33.4 us  [swap(): return lax.all_to_all(x, axis, 0, 0, tiled=True)]
    ppermute x1 -> x0, starting transfers between devices: 1.92 us -> none  [per_device(): other = lax.ppermute(send, 'core', [(0, 1), (1, 0)])]
  transfers between devices with their start and end apart: 4 -> 3, of which waited for: 2 -> 1; matrix products, arithmetic and copies ran while one was open for 0% -> 0% of each run, Pallas kernels for 2% -> 2%
where the time goes in v5:
time: 106 us
  blocking collectives  56.2 us (53%)
  starting transfers between devices  33.4 us (32%)
  Pallas kernels  7.48 us (7%)
  waiting for transfers between devices  6.51 us (6%)
  between operations  1.34 us (1%)
    all_to_all x3, starting transfers between devices, swap(): return lax.all_to_all(x, axis, 0, 0, tiled=True)  33.4 us
    all_to_all x1, blocking collectives, swap(): return lax.all_to_all(x, axis, 0, 0, tiled=True)  17.8 us
    all_gather x1, blocking collectives, per_device(): parts = lax.all_gather(part, 'item', axis=0)  14.9 us
    all_gather x1, blocking collectives, per_device(): lax.all_gather(part, 'item', axis=0, axis_index_groups=[[0, 1], [2, 3]])  11.4 us
    all_to_all x3, waiting for transfers between devices, swap(): return lax.all_to_all(x, axis, 0, 0, tiled=True)  6.51 us
    all_gather x1, blocking collectives, per_device(): lax.all_gather(pair, 'item', axis=0, axis_index_groups=[[0, 3], [1, 2]])  5.63 us
    all_gather x1, blocking collectives, per_device(): item_one = lax.all_gather(half.reshape(-1, DIM), 'core', axis=0, tiled=True)  2.18 us
    all_gather x1, blocking collectives, per_device(): sent = lax.all_gather(send, 'core', axis=0)  2.18 us
  transfers between devices with their start and end apart: 3, of which 1 were waited for; matrix products, arithmetic and copies ran while one was open for 0% of the time, Pallas kernels for 2%

profile of v5, /device:TPU:10, one launch (start us, length us, event | category | flops | bytes accessed | tf_op | source)
XLA Modules:
  0.0 105.7 jit_solution(4162260186966240468)
XLA Ops:
  1.3 2.0 %first.1 = (bf16[512,2048]{1,0:T(8,128)(2,1)S(1)}, bf16[2048,128]{1,0:T(8,128)(2,1)S(1)}, bf16[512,128]{1,0:T(8,128)(2,1)S(1)}) custom-call(s32[1]{0:T(128)S(6)} %copy.11.count_ref, s32[48]{0:T(128)} %tu_hbm.1, s32[48]{0:T(128)} %ti_hbm.1, bf16[48,128,128]{2,1,0:T(8,128)(2,1)} %tiles_hbm.1, bf16[2048,128]{1,0:T(8,128)(2,1)} %emb_ref.1, bf16[512,128]{1,0:T(8,128)(2,1)} %user_ref.1), custom_call_target="tpu_custom_call" | custom-call | tf_op jit(solution)/shard_map/first/pallas_call | solution.py:84
  3.3 0.9 back.1
  4.2 2.2 %all-gather = bf16[32,64,128]{2,1,0:T(8,128)(2,1)S(1)} all-gather(bf16[16,64,128]{2,1,0:T(8,128)(2,1)S(1)} %get-tuple-element.22), channel_id=2, replica_groups=mesh['zh'=8,'zl'=2,'y'=8,'core'=2,'item'=4] {'core'}, dimensions={0}, use_global_device_ids=true | all-gather | bytes 786432 | tf_op jit(solution)/shard_map/all_gather | solution.py:282
  6.4 0.8 join.1
  7.1 9.8 %all-to-all-start = ((bf16[16,64,128]{2,1,0:T(8,128)(2,1)}), bf16[16,64,128]{2,1,0:T(8,128)(2,1)S(1)}, u32[]{:S(2)}, u32[]{:S(2)}) async-start(bf16[16,64,128]{2,1,0:T(8,128)(2,1)} %join.1), calls=%async_computation | async-start | bytes 524288 | tf_op jit(solution)/shard_map/all_to_all | solution.py:272
  16.9 0.7 part.1
  17.6 11.4 %all-gather.1 = bf16[1024,128]{1,0:T(8,128)(2,1)S(1)} all-gather(bf16[512,128]{1,0:T(8,128)(2,1)S(1)} %part.1), channel_id=3, replica_groups={{0,1},{2,3},{4,5},{6,7},{8,9},{10,11},{12,13},{14,15},{16,17},{18,19},{..., dimensions={0}, use_global_device_ids=true | all-gather | bytes 393216 | tf_op jit(solution)/shard_map/all_gather | solution.py:286
  29.0 0.0 all-to-all-done
  29.1 0.7 broadcast_in_dim.2
  29.8 15.6 %all-to-all-start.1 = ((bf16[8,64,128]{2,1,0:T(8,128)(2,1)}), bf16[8,64,128]{2,1,0:T(8,128)(2,1)S(1)}, u32[]{:S(2)}, u32[]{:S(2)}) async-start(bf16[8,64,128]{2,1,0:T(8,128)(2,1)} %broadcast_in_dim.2), calls=%async_computation.1 | async-start | bytes 262144 | tf_op jit(solution)/shard_map/all_to_all | solution.py:272
  45.4 5.6 %all-gather.2 = bf16[1024,128]{1,0:T(8,128)(2,1)S(1)} all-gather(bf16[512,128]{1,0:T(8,128)(2,1)S(1)} %reduce_sum.24), channel_id=4, replica_groups={{0,3},{1,2},{4,7},{5,6},{8,11},{9,10},{12,15},{13,14},{16,19},{17,18},{..., dimensions={0}, use_global_device_ids=true | all-gather | bytes 393216 | tf_op jit(solution)/shard_map/all_gather | solution.py:294
  51.0 1.0 second.1
  52.0 2.2 %all-gather.3 = bf16[32,64,128]{2,1,0:T(8,128)(2,1)S(1)} all-gather(bf16[16,64,128]{2,1,0:T(8,128)(2,1)S(1)} %get-tuple-element.32), channel_id=5, replica_groups=mesh['zh'=8,'zl'=2,'y'=8,'core'=2,'item'=4] {'core'}, dimensions={0}, use_global_device_ids=true | all-gather | bytes 786432 | tf_op jit(solution)/shard_map/all_gather | solution.py:296
  54.2 6.5 %all-to-all-done.1.got_ref = bf16[8,64,128]{2,1,0:T(8,128)(2,1)S(1)} async-done(((bf16[8,64,128]{2,1,0:T(8,128)(2,1)}), bf16[8,64,128]{2,1,0:T(8,128)(2,1)S(1)}, u32[]{:S(2)}, u32[]{:S(2)}) %all-to-all-start.1) | async-done | bytes 131104 | tf_op jit(solution)/shard_map/all_to_all | solution.py:272
  60.7 0.0 copy-start
  60.7 0.1 spread.1
  60.8 17.8 %all_to_all.20 = bf16[16,2,64,128]{3,2,1,0:T(8,128)(2,1)S(1)} all-to-all(bf16[16,2,64,128]{3,2,1,0:T(8,128)(2,1)S(1)} %spread.1), channel_id=1, replica_groups=mesh['zh'=8,'zl'=2,'y'=8,'core'=2,'item'=4] {'zl','y'}, dimensions={0} | all-to-all | bytes 1048576 | tf_op jit(solution)/shard_map/all_to_all | solution.py:272
  78.6 2.2 %all_gather.41.one_ref = bf16[2048,128]{1,0:T(8,128)(2,1)S(1)} all-gather(bf16[1024,128]{1,0:T(8,128)(2,1)S(1)} %bitcast.16), channel_id=1, replica_groups=mesh['zh'=8,'zl'=2,'y'=8,'core'=2,'item'=4] {'core'}, dimensions={0}, use_global_device_ids=true | all-gather | bytes 786432 | tf_op jit(solution)/shard_map/all_gather | solution.py:300
  80.8 0.0 copy-start.1
  80.8 0.0 copy-start.2
  80.8 0.0 copy-done
  80.8 1.3 %third.1 = (bf16[512,128]{1,0:T(8,128)(2,1)S(1)}, f32[8,128]{1,0:T(8,128)S(1)}, bf16[64,128]{1,0:T(8,128)(2,1)}) custom-call(bf16[512,2048]{1,0:T(8,128)(2,1)S(1)} %get-tuple-element.19.r_ref, bf16[2048,128]{1,0:T(8,128)(2,1)S(1)} %all_gather.41.one_ref, bf16[2048,128]{1,0:T(8,128)(2,1)S(1)} %copy-done, bf16[16,64,128]{2,1,0:T(8,128)(2,1)S(1)} %get-tuple-element.36.back_ref), custom_call_target="tpu_custom_call" | custom-call | tf_op jit(solution)/shard_map/third/pallas_call | solution.py:234
  82.1 8.0 %all-to-all-start.3 = ((bf16[8,8,128]{2,1,0:T(8,128)(2,1)}), bf16[8,8,128]{2,1,0:T(8,128)(2,1)S(1)}, u32[]{:S(2)}, u32[]{:S(2)}) async-start(bf16[8,8,128]{2,1,0:T(8,128)(2,1)} %bitcast.7), calls=%async_computation.3 | async-start | bytes 32768 | tf_op jit(solution)/shard_map/all_to_all | solution.py:272
  90.1 14.9 %all-gather.4 = bf16[2048,128]{1,0:T(8,128)(2,1)S(1)} all-gather(bf16[512,128]{1,0:T(8,128)(2,1)S(1)} %get-tuple-element.33), channel_id=6, replica_groups=mesh['zh'=8,'zl'=2,'y'=8,'core'=2,'item'=4] {'item'}, dimensions={0}, use_global_device_ids=true | all-gather | bytes 655360 | tf_op jit(solution)/shard_map/all_gather | solution.py:303
  105.0 0.0 all-to-all-done.3.two_ref
  105.0 0.0 copy-done.1
  105.0 0.0 copy-done.2
  105.0 0.8 last.1
  (3 shorter events, 0.1 us)
Async XLA Ops:
  7.1 21.9 %all-to-all-start = ((bf16[16,64,128]{2,1,0:T(8,128)(2,1)}), bf16[16,64,128]{2,1,0:T(8,128)(2,1)S(1)}, u32[]{:S(2)}, u32[]{:S(2)}) async-start(bf16[16,64,128]{2,1,0:T(8,128)(2,1)} %join.1), calls=%async_computation | async-start | bytes 524288 | tf_op jit(solution)/shard_map/all_to_all | solution.py:272
  29.8 30.9 %all-to-all-start.1 = ((bf16[8,64,128]{2,1,0:T(8,128)(2,1)}), bf16[8,64,128]{2,1,0:T(8,128)(2,1)S(1)}, u32[]{:S(2)}, u32[]{:S(2)}) async-start(bf16[8,64,128]{2,1,0:T(8,128)(2,1)} %broadcast_in_dim.2), calls=%async_computation.1 | async-start | bytes 262144 | tf_op jit(solution)/shard_map/all_to_all | solution.py:272
  60.7 20.1 %copy-start = (bf16[2048,128]{1,0:T(8,128)(2,1)S(1)}, bf16[2048,128]{1,0:T(8,128)(2,1)}, u32[]{:S(2)}) copy-start(bf16[2048,128]{1,0:T(8,128)(2,1)} %emb_ref.1) | copy-start | bytes 1572868
  80.8 24.2 %copy-start.1 = (bf16[512,128]{1,0:T(8,128)(2,1)S(1)}, bf16[512,128]{1,0:T(8,128)(2,1)}, u32[]{:S(2)}) copy-start(bf16[512,128]{1,0:T(8,128)(2,1)} %user_ref.1) | copy-start | bytes 393220
  80.8 24.2 %copy-start.2 = (bf16[512,128]{1,0:T(8,128)(2,1)S(1)}, bf16[512,128]{1,0:T(8,128)(2,1)}, u32[]{:S(2)}) copy-start(bf16[512,128]{1,0:T(8,128)(2,1)} %get-tuple-element.29.one_ref) | copy-start | bytes 393220
  82.1 22.9 %all-to-all-start.3 = ((bf16[8,8,128]{2,1,0:T(8,128)(2,1)}), bf16[8,8,128]{2,1,0:T(8,128)(2,1)S(1)}, u32[]{:S(2)}, u32[]{:S(2)}) async-start(bf16[8,8,128]{2,1,0:T(8,128)(2,1)} %bitcast.7), calls=%async_computation.3 | async-start | bytes 32768 | tf_op jit(solution)/shard_map/all_to_all | solution.py:272
